TPU v7x, 256 devices: a whole 4x4x8 slice. The times are simulated.
256 devices in a mesh: dp: 16 (over x, y), enc: 16 (over z, core).
Axes of the slice: x: 4, y: 4, z: 8, core: 2. Of those that a mesh axis runs over, the one named last changes fastest.
Arguments:
- targets: bfloat16 [16384, 4096], P('enc', 'dp'), may hold values from -6 to 6
- encoded: bfloat16 [2048, 4096], P('enc', 'dp'), may hold values from -70 to 70
- norm_gain: float32 [4096], replicated, may hold values from 0.1 to 1.9
- query_weight: bfloat16 [4096, 4096], P(None, 'dp'), may hold values from -0.005859375 to 0.005859375
- key_weight: bfloat16 [4096, 4096], P(None, 'dp'), may hold values from -0.09375 to 0.09375
- value_weight: bfloat16 [4096, 4096], P(None, 'dp'), may hold values from -0.09375 to 0.09375
- output_weight: bfloat16 [4096, 4096], P('dp'), may hold values from -0.09375 to 0.09375
- target_segment: int32 [16384], replicated, may hold values from 0 to 63, never falling along the last dimension, each value on 1 to 512 neighbouring positions
- encoder_segment: int32 [2048], replicated, may hold values from 0 to 63, as said below
- tile_slot: int32 [128], replicated, may hold values from 0 to 127, as said below
Outputs:
- attended: bfloat16 [16384, 4096], P('enc', 'dp')
Inputs may be any that keep to these rules, and one draw needn't show every extreme that they name: `target_segment`: never falling; every segment 0 to 63 holds target tokens and encoder tokens both; some segment has exactly 512 target tokens. `encoder_segment`: each segment's encoder tokens stand together in one run, every segment has one; some segment has exactly 256 encoder tokens. `tile_slot`: each slot once; the 8 tiles of one index of enc go to 8 different owners, so every owner receives exactly one tile from each of 8 different indices of enc.
All inputs are finite; a program needn't handle non-finite values.
Results may differ from a plain program's by a relative error of at most 0.019.
Values may be sent and summed in bfloat16 or wider, within the bound.
A program may use at most 128 MiB of HBM per device.

v0:
```python
import jax
import jax.numpy as jnp
from jax import lax
from jax.sharding import PartitionSpec as P

HD = 256
TILE = 128


def attend(query_rows, query_segment, key_value, encoder_segment):
    row_count = query_rows.shape[0]
    head_count = query_rows.shape[1] // HD
    head_queries = query_rows.reshape(row_count, head_count, HD)
    tile_segment = query_segment.reshape(-1, TILE)
    lowest = tile_segment[:, 0]
    highest = tile_segment[:, TILE - 1]
    start_state = (
        jnp.full((head_count, row_count), -1e30, jnp.float32),
        jnp.zeros((head_count, row_count), jnp.float32),
        jnp.zeros((head_count, row_count, HD), jnp.float32),
    )
    piece_block = lax.all_gather(key_value, "enc", axis=0, tiled=True)
    block_rows = piece_block.shape[0]
    needed = jnp.any((lowest <= jnp.max(encoder_segment)) & (highest >= jnp.min(encoder_segment)))

    def update(old_state):
        run_max, denominator, accumulated = old_state
        key_block = piece_block[:, : head_count * HD].reshape(block_rows, head_count, HD)
        value_block = piece_block[:, head_count * HD :].reshape(block_rows, head_count, HD)
        scores = jnp.einsum(
            "rhd,khd->hrk", head_queries, key_block, preferred_element_type=jnp.float32
        )
        allowed = (query_segment[:, None] == encoder_segment[None, :])[None]
        scores = jnp.where(allowed, scores, -1e30)
        new_max = jnp.maximum(run_max, jnp.max(scores, axis=-1))
        weights = jnp.where(allowed, jnp.exp(scores - new_max[..., None]), 0.0)
        denominator = jnp.sum(weights, axis=-1)
        accumulated = jnp.einsum(
            "hrk,khd->hrd",
            weights.astype(jnp.bfloat16),
            value_block,
            preferred_element_type=jnp.float32,
        )
        return (new_max, denominator, accumulated)

    def unchanged(old_state):
        return old_state

    run_max, denominator, accumulated = lax.cond(needed, update, unchanged, start_state)
    context = accumulated / denominator[..., None]
    return (
        jnp.transpose(context, (1, 0, 2)).reshape(row_count, head_count * HD).astype(jnp.bfloat16)
    )


def outgoing_tiles(local_rows, send_match, enc_count):
    width = local_rows.shape[1]
    stacked = local_rows.reshape(send_match.shape[1], TILE * width)
    placed = jnp.dot(send_match, stacked, preferred_element_type=jnp.float32).astype(jnp.bfloat16)
    return placed.reshape(enc_count, TILE, width)


def arrived_tiles(incoming, pick_rows):
    enc_count, tile_rows, width = incoming.shape
    flat = incoming.reshape(enc_count, tile_rows * width)
    chosen = jnp.dot(pick_rows, flat, preferred_element_type=jnp.float32).astype(jnp.bfloat16)
    return chosen.reshape(pick_rows.shape[0] * tile_rows, width)


def local(
    targets,
    encoded,
    norm_gain,
    query_weight,
    key_weight,
    value_weight,
    output_weight,
    target_segment,
    encoder_segment,
    tile_slot,
):
    whole_targets, whole_encoded = (
        lax.all_gather(targets, "dp", axis=1, tiled=True),
        lax.all_gather(encoded, "dp", axis=1, tiled=True),
    )
    widened = whole_targets.astype(jnp.float32)
    inverse_rms = lax.rsqrt(jnp.mean(widened * widened, axis=-1, keepdims=True) + 1e-06)
    normed = (widened * inverse_rms * norm_gain).astype(jnp.bfloat16)
    queries = jnp.dot(normed, query_weight, preferred_element_type=jnp.float32).astype(jnp.bfloat16)
    key_value = jnp.concatenate(
        (
            jnp.dot(whole_encoded, key_weight, preferred_element_type=jnp.float32),
            jnp.dot(whole_encoded, value_weight, preferred_element_type=jnp.float32),
        ),
        axis=1,
    ).astype(jnp.bfloat16)
    tile_total = tile_slot.shape[0]
    tiles_here = queries.shape[0] // TILE
    enc_count = lax.axis_size("enc")
    position = lax.axis_index("enc")
    home_tiles = position * tiles_here + jnp.arange(tiles_here, dtype=jnp.int32)
    slot_match = tile_slot[:, None] == home_tiles[None, :]
    source_tile = jnp.sum(
        jnp.where(slot_match, jnp.arange(tile_total, dtype=jnp.int32)[:, None], 0), axis=0
    )
    home_owner = tile_slot[home_tiles] // tiles_here
    peers = jnp.arange(enc_count, dtype=jnp.int32)
    send_match = (peers[:, None] == home_owner[None, :]).astype(jnp.bfloat16)
    pick_rows = ((source_tile // tiles_here)[:, None] == peers[None, :]).astype(jnp.bfloat16)
    segment_tiles = target_segment.reshape(tile_total, TILE)
    home_context = attend(
        queries, segment_tiles[home_tiles].reshape(-1), key_value, encoder_segment
    )
    incoming = lax.all_to_all(
        outgoing_tiles(home_context, send_match, enc_count),
        "enc",
        split_axis=0,
        concat_axis=0,
        tiled=True,
    )
    context = arrived_tiles(incoming, pick_rows)
    partial_out = jnp.dot(context, output_weight, preferred_element_type=jnp.float32)
    projected = lax.psum_scatter(
        partial_out.astype(jnp.bfloat16), "dp", scatter_dimension=1, tiled=True
    )
    return projected


def solution(mesh):
    return jax.shard_map(
        local,
        mesh=mesh,
        in_specs=(
            P("enc", "dp"),
            P("enc", "dp"),
            P(),
            P(None, "dp"),
            P(None, "dp"),
            P(None, "dp"),
            P("dp", None),
            P(),
            P(),
            P(),
        ),
        out_specs=P("enc", "dp"),
        check_vma=False,
    )
```

profile of v0, /device:TPU:8, one launch (start us, length us, event | category | flops | bytes accessed | tf_op | source)
XLA Modules:
  0.0 331.7 jit_solution(6679822116432118196)
XLA Ops:
  6.5 0.0 copy-start
  6.5 0.0 copy-start.5
  6.5 0.0 all-gather.4.cloned.1.call-start
  6.5 0.7 all-gather.4.cloned.1.call-update
  7.3 0.0 all-gather.8.cloned.1.call-start
  7.3 0.7 all-gather.8.cloned.1.call-update
  8.0 0.0 all-gather.6.cloned.1.call-start
  8.1 52.6 %all-gather.4.cloned.1.call-done = bf16[128,4096]{1,0:T(8,128)(2,1)} async-done(((bf16[128,256]{1,0:T(8,128)(2,1)}), bf16[128,4096]{1,0:T(8,128)(2,1)}) %all-gather.4.cloned.1.call-update) | async-done | bytes 1048592 | tf_op jit(solution)/shard_map/all_gather | solution.py:84
  60.7 2.4 convolution_convert_fusion.3
  63.0 2.4 convolution_convert_fusion.4
  65.4 0.7 pad_maximum_fusion
  66.1 0.0 all-gather.6.cloned.1.call-update
  66.1 1.3 gather_fusion
  67.4 1.4 gather_fusion.1
  68.8 1.3 fusion.28
  70.2 1.9 fusion.25
  72.7 73.2 %all-gather.8.cloned.1.call-done = bf16[1024,4096]{1,0:T(8,128)(2,1)} async-done(((bf16[1024,256]{1,0:T(8,128)(2,1)}), bf16[1024,4096]{1,0:T(8,128)(2,1)}) %all-gather.8.cloned.1.call-update) | async-done | bytes 8388624 | tf_op jit(solution)/shard_map/all_gather | solution.py:83
  145.9 0.0 copy-start.2
  145.9 5.2 %fusion.13 = f32[1024]{0:T(1024)S(1)} fusion(bf16[1024,4096]{1,0:T(8,128)(2,1)} %all-gather.8.cloned.1.call-done), kind=kLoop, calls=%fused_computation.19 | loop fusion | flops 12581888 | bytes 8392704 | tf_op jit(solution)/shard_map/reduce_sum | solution.py:87
  151.2 0.0 copy-done.5
  151.2 0.5 copy-done.2
  151.7 0.0 copy-start.3
  151.7 4.9 %fusion.20 = bf16[1024,256]{1,0:T(8,128)(2,1)} fusion(bf16[4096,256]{1,0:T(8,128)(2,1)} %param.15, bf16[1024,4096]{1,0:T(8,128)(2,1)S(1)} %copy-done.2, f32[4096]{0:T(1024)S(1)} %copy-done.5, f32[1024]{0:T(1024)S(1)} %add_rsqrt_fusion), kind=kOutput, calls=%fused_computation.26 | convolution fusion | flops 2164523008 | bytes 11030528 | tf_op jit(solution)/shard_map/dot_general | solution.py:89
  156.5 30.8 %all-gather.6.cloned.1.call-done = bf16[2048,512]{1,0:T(8,128)(2,1)} async-done(((bf16[128,512]{1,0:T(8,128)(2,1)}), bf16[2048,512]{1,0:T(8,128)(2,1)}) %all-gather.6.cloned.1.call-update) | async-done | bytes 2097168 | tf_op jit(solution)/shard_map/all_gather | solution.py:22
  187.3 0.0 copy-done.3
  187.3 7.3 %conditional.1 = (f32[1,1024]{1,0:T(1,128)S(1)}, f32[1,1024,256]{2,1,0:T(8,128)S(1)}) conditional(s32[]{:T(128)} %convert_element_type.35, () %tuple.13, (s32[8,128]{1,0:T(8,128)S(1)}, s32[2048]{0:T(1024)S(1)}, bf16[2048,512]{1,0:T(8,128)(2,1)}, bf16[1024,256]{1,0:T(8,128)(2,1)}) %tuple.27), branch_computations={%region_5.6_spmd, %region_6.9_spmd} | conditional | flops 2174745600 | bytes 37285932 | solution.py:49
  187.3 0.0 copy-start.4
  187.3 2.9 fusion
  190.3 0.0 copy-done.4
  190.3 1.8 fusion.5
  192.1 2.6 fusion.2
  194.7 0.0 copy-start.1
  194.7 1.0 divide_convert_fusion
  195.7 1.3 convert_element_type.40
  197.0 0.4 convolution_convert_fusion
  197.4 1.2 copy.11
  198.6 4.1 %all-to-all-start = ((bf16[16,128,256]{2,1,0:T(8,128)(2,1)}), bf16[16,128,256]{2,1,0:T(8,128)(2,1)S(1)}, u32[]{:S(2)}, u32[]{:S(2)}) async-start(bf16[16,128,256]{2,1,0:T(8,128)(2,1)} %bitcast.23), calls=%async_computation | async-start | bytes 2097152 | tf_op jit(solution)/shard_map/all_to_all | solution.py:114
  202.7 0.2 reduce-scatter.2.cloned.1.call-start
  203.0 0.0 copy-done.1
  203.0 0.2 select_reduce_fusion
  203.2 26.2 %all-to-all-done = bf16[16,128,256]{2,1,0:T(8,128)(2,1)S(1)} async-done(((bf16[16,128,256]{2,1,0:T(8,128)(2,1)}), bf16[16,128,256]{2,1,0:T(8,128)(2,1)S(1)}, u32[]{:S(2)}, u32[]{:S(2)}) %all-to-all-start) | async-done | bytes 1048608 | tf_op jit(solution)/shard_map/all_to_all | solution.py:114
  229.4 0.6 copy.12
  230.0 0.4 convolution_convert_fusion.1
  230.3 0.2 reshape.121
  230.6 0.0 copy-done
  230.6 5.6 %convolution_convert_fusion.2 = bf16[1024,4096]{1,0:T(8,128)(2,1)} fusion(bf16[1024,256]{1,0:T(8,128)(2,1)S(1)} %reshape.121, bf16[256,4096]{1,0:T(8,128)(2,1)S(1)} %copy-done), kind=kOutput, calls=%fused_computation.25 | convolution fusion | flops 2151677952 | bytes 11010048 | tf_op jit(solution)/shard_map/dot_general | solution.py:122
  236.2 0.0 reduce-scatter.2.cloned.1.call-update
  236.2 88.9 %reduce-scatter.2.cloned.1.call-done = bf16[1024,256]{1,0:T(8,128)(2,1)} async-done(((bf16[1024,4096]{1,0:T(8,128)(2,1)}), bf16[1024,256]{1,0:T(8,128)(2,1)}) %reduce-scatter.2.cloned.1.call-update) | async-done | bytes 524304 | tf_op jit(solution)/shard_map/reduce_scatter | solution.py:123
  (7 shorter events, 0.1 us)
Async XLA Ops:
  6.5 224.1 %copy-start = (bf16[256,4096]{1,0:T(8,128)(2,1)S(1)}, bf16[256,4096]{1,0:T(8,128)(2,1)}, u32[]{:S(2)}) copy-start(bf16[256,4096]{1,0:T(8,128)(2,1)} %param.18) | copy-start | bytes 6291460
  6.5 144.6 %copy-start.5 = (f32[4096]{0:T(1024)S(1)}, f32[4096]{0:T(1024)}, u32[]{:S(2)}) copy-start(f32[4096]{0:T(1024)} %param.14) | copy-start | bytes 49156
  6.5 54.1 %all-gather.4.cloned.1.call-start = ((), (), s32[]{:S(2)}) async-start(), calls=%async_computation.2 | async-start | bytes 1114112 | tf_op jit(solution)/shard_map/all_gather | solution.py:84
  7.3 138.7 %all-gather.8.cloned.1.call-start = ((), (), s32[]{:S(2)}) async-start(), calls=%async_computation.4 | async-start | bytes 8912896 | tf_op jit(solution)/shard_map/all_gather | solution.py:83
  8.0 179.3 %all-gather.6.cloned.1.call-start = ((), (), s32[]{:S(2)}) async-start(), calls=%async_computation.3 | async-start | bytes 2228224 | tf_op jit(solution)/shard_map/all_gather | solution.py:22
  145.9 5.8 %copy-start.2 = (bf16[1024,4096]{1,0:T(8,128)(2,1)S(1)}, bf16[1024,4096]{1,0:T(8,128)(2,1)}, u32[]{:S(2)}) copy-start(bf16[1024,4096]{1,0:T(8,128)(2,1)} %all-gather.8.cloned.1.call-done) | copy-start | bytes 25165828
  151.7 35.6 %copy-start.3 = (s32[2048]{0:T(1024)S(1)}, s32[2048]{0:T(1024)}, u32[]{:S(2)}) copy-start(s32[2048]{0:T(1024)} %param.20) | copy-start | bytes 24580
  187.3 2.9 copy-start.4
  194.7 8.3 %copy-start.1 = (s32[128]{0:T(128)S(1)}, s32[128]{0:T(128)}, u32[]{:S(2)}) copy-start(s32[128]{0:T(128)} %param.21) | copy-start | bytes 1540
  198.6 30.8 %all-to-all-start = ((bf16[16,128,256]{2,1,0:T(8,128)(2,1)}), bf16[16,128,256]{2,1,0:T(8,128)(2,1)S(1)}, u32[]{:S(2)}, u32[]{:S(2)}) async-start(bf16[16,128,256]{2,1,0:T(8,128)(2,1)} %bitcast.23), calls=%async_computation | async-start | bytes 2097152 | tf_op jit(solution)/shard_map/all_to_all | solution.py:114
  202.7 122.4 %reduce-scatter.2.cloned.1.call-start = ((), (), s32[]{:S(2)}) async-start(), calls=%async_computation.5 | async-start | bytes 8912896 | tf_op jit(solution)/shard_map/reduce_scatter | solution.py:123
Sparse Core Ops, SparseCore 0:
  9.8 50.8 all-gather.3
  63.1 82.8 all-gather.7
  147.8 39.5 all-gather.5
  236.3 88.7 reduce-scatter.1
where the time goes:
time: 332 us
  waiting for transfers between devices  273 us (82%)
  matrix products  20.6 us (6%)
  between operations  13.8 us (4%)
  other arithmetic  13 us (4%)
  local copies, waits for them, and re-layouts  6.57 us (2%)
  starting transfers between devices  4.43 us (1%)
    reduce_scatter x1, waiting for transfers between devices, local(): lax.psum_scatter(partial_out.astype(jnp.bfloat16), 'dp', scatter_dimensio...  88.9 us
    all_gather x1, waiting for transfers between devices, local(): lax.all_gather(targets, 'dp', axis=1, tiled=True)  73.2 us
    all_gather x1, waiting for transfers between devices, local(): lax.all_gather(encoded, 'dp', axis=1, tiled=True)  52.6 us
    all_gather x1, waiting for transfers between devices, attend(): piece_block = lax.all_gather(key_value, 'enc', axis=0, tiled=True)  30.8 us
    all_to_all x1, waiting for transfers between devices, local(): lax.all_to_all(outgoing_tiles(home_context, send_match, enc_count), 'enc'...  26.2 us
  transfers between devices with their start and end apart: 5, of which 5 were waited for; matrix products, arithmetic and copies ran while one was open for 7% of the time, Pallas kernels for 0%

commit v1 on v0

v1 whole, which is shorter than its diff:
```python
import jax
import jax.numpy as jnp
from jax import lax
from jax.experimental import pallas as pl
from jax.experimental.pallas import tpu as pltpu
from jax.sharding import PartitionSpec as P

HD = 256
TILE = 128
TILES = 8
HALF = TILE // 2
SIDE = 4
DEPTH = 8
ENC_PEERS = 16
FEATURES = 4096
BF = jnp.bfloat16
F32 = jnp.float32


def kernel(
    targets,
    encoded,
    gain,
    query_weight,
    key_weight,
    value_weight,
    output_weight,
    target_segment,
    encoder_segment,
    slot_row,
    slot,
    out,
    own_targets,
    sent_tiles,
    came_tiles,
    enc_all,
    weight_k,
    weight_v,
    weight_q,
    weight_o,
    kv,
    squares,
    rows_q,
    rows_o,
    kept_q,
    kept_o,
    far_q,
    far_o,
    half_q,
    half_o,
    near_q,
    near_o,
    sum_q,
    sum_o,
    out_rows,
    local_sem,
    enc_sem,
    tile_sem,
    wq_sem,
    wo_sem,
    pair_sem,
    kv_sem,
    kvp_sem,
    sq_sem,
    gather_q_sem,
    gather_o_sem,
    pass_q_sem,
    pass_o_sem,
    far_q_sem,
    far_o_sem,
    near_q_sem,
    near_o_sem,
    out_sem,
):
    dp = lax.axis_index("dp")
    e = lax.axis_index("enc")
    x, y = dp // SIDE, dp % SIDE
    z, c = e // 2, e % 2

    def device(dx=0, dy=0, dz=0, dc=0):
        return (
            ((x + dx + SIDE) % SIDE) * SIDE + (y + dy + SIDE) % SIDE,
            ((z + dz + DEPTH) % DEPTH) * 2 + (c + dc) % 2,
        )

    def remote(src, dst, sems, index, to):
        return pltpu.make_async_remote_copy(
            src_ref=src,
            dst_ref=dst,
            send_sem=sems.at[(0,) + index],
            recv_sem=sems.at[(1,) + index],
            device_id=to,
            device_id_type=pl.DeviceIdType.MESH,
        )

    right_x, left_x = (x + 1) % SIDE, (x + 3) % SIDE
    far_x = (x + 2) % SIDE
    dp_steps = [(i, j) for i in (2, 1, 3, 0) for j in (2, 1, 3, 0) if (i, j) != (0, 0)]
    enc_steps = [(i, j) for i in (4, 3, 5, 2, 6, 1, 7, 0) for j in (0, 1) if (i, j) != (0, 0)]

    load_targets = pltpu.make_async_copy(targets, own_targets, local_sem.at[0])
    load_encoded = pltpu.make_async_copy(encoded, enc_all.at[dp], local_sem.at[1])
    load_k = pltpu.make_async_copy(key_weight, weight_k, local_sem.at[2])
    load_v = pltpu.make_async_copy(value_weight, weight_v, local_sem.at[3])
    load_q = pltpu.make_async_copy(query_weight.at[:, y], weight_q.at[y], local_sem.at[4])
    load_o = pltpu.make_async_copy(
        output_weight.at[:, pl.ds(pl.multiple_of(x * 1024, 1024), 1024)],
        weight_o.at[x],
        local_sem.at[5],
    )
    load_targets.start()
    load_encoded.start()
    load_k.start()
    load_v.start()
    load_q.start()
    load_o.start()

    barrier = pltpu.get_barrier_semaphore()
    for i, j in dp_steps:
        pl.semaphore_signal(
            barrier, inc=1, device_id=device(dx=i, dy=j), device_id_type=pl.DeviceIdType.MESH
        )
    for i, j in enc_steps:
        pl.semaphore_signal(
            barrier, inc=1, device_id=device(dz=i, dc=j), device_id_type=pl.DeviceIdType.MESH
        )
    pl.semaphore_wait(barrier, len(dp_steps) + len(enc_steps))

    def enc_copy(i, j):
        return remote(
            encoded, enc_all.at[dp], enc_sem, (i * SIDE + j,), device(dx=i, dy=j)
        )

    for i, j in dp_steps:
        enc_copy(i, j).start()

    load_targets.wait()
    owners = [slot[e * TILES + i] // TILES for i in range(TILES)]

    def tile_copy(i, j):
        to = device(dz=i, dc=j)
        return to[1], remote(
            sent_tiles.at[i * 2 + j], came_tiles.at[e], tile_sem, (i * 2 + j,), to
        )

    def tile_for(peer):
        found = jnp.int32(0)
        for i in range(1, TILES):
            found = jnp.where(owners[i] == peer, i, found)
        return own_targets[found]

    for i, j in enc_steps:
        peer, copy = tile_copy(i, j)
        sent_tiles[i * 2 + j] = tile_for(peer)
        copy.start()
    came_tiles[e] = tile_for(e)

    def wq_copy(j):
        part = pl.ds(2 * c, 2)
        return remote(
            query_weight.at[part, (y + j) % SIDE],
            weight_q.at[y, part],
            wq_sem,
            (j,),
            device(dy=j),
        )

    def wo_copy(i):
        part = pl.ds(pl.multiple_of(c * TILE, TILE), TILE)
        return remote(
            output_weight.at[part, pl.ds(pl.multiple_of(((x + i) % SIDE) * 1024, 1024), 1024)],
            weight_o.at[x, part],
            wo_sem,
            (i,),
            device(dx=i),
        )

    for i in (2, 1, 3):
        wq_copy(i).start()
    for i in (2, 1, 3):
        wo_copy(i).start()

    load_encoded.wait()
    for i, j in dp_steps:
        enc_copy(i, j).wait()
    load_k.wait()
    load_v.wait()

    def project(block, sums):
        rows = enc_all[block]
        return (
            sums[0] + jnp.dot(rows, weight_k[block], preferred_element_type=F32),
            sums[1] + jnp.dot(rows, weight_v[block], preferred_element_type=F32),
        )

    zero = jnp.zeros((TILE, HD), F32)
    key_rows, value_rows = lax.fori_loop(0, ENC_PEERS, project, (zero, zero))
    kv[e, 0] = key_rows.astype(BF)
    kv[e, 1] = value_rows.astype(BF)

    def kv_block(step):
        return ((z + step + DEPTH) % DEPTH) * 2 + c

    def kv_copy(step, way):
        block = kv_block(-step * way)
        return remote(
            kv.at[block],
            kv.at[block],
            kv_sem,
            (step, 0 if way > 0 else 1),
            device(dz=way),
        )

    def kv_last(way):
        block = kv_block(-3 * way)
        part = 0 if way > 0 else 1
        return remote(
            kv.at[block, part], kv.at[block, part], kv_sem, (3, part), device(dz=way)
        )

    def kv_pair(step):
        block = kv_block(step)
        return remote(kv.at[block], kv.at[block], kvp_sem, ((step + DEPTH) % DEPTH,), device(dc=1))

    kv_copy(0, 1).start()
    kv_copy(0, -1).start()
    kv_pair(0).start()

    def wq_pair(j):
        block = (y + SIDE - j) % SIDE
        part = pl.ds(2 * c, 2)
        ref = weight_q.at[block, part]
        return remote(ref, ref, pair_sem, (j,), device(dc=1))

    def wo_pair(i):
        block = (x + SIDE - i) % SIDE
        part = pl.ds(pl.multiple_of(c * TILE, TILE), TILE)
        ref = weight_o.at[block, part]
        return remote(ref, ref, pair_sem, (SIDE + i,), device(dc=1))

    for i in (1, 3, 2):
        wq_copy(i).wait()
        wq_pair(i).start()

    for i, j in enc_steps:
        tile_copy(i, j)[1].wait()

    lanes = lax.broadcasted_iota(jnp.int32, (TILE, TILE), 1)
    eye = lax.broadcasted_iota(jnp.int32, (TILE, TILE), 0) == lanes

    def to_row(column):
        return jnp.sum(jnp.where(eye, column, 0.0), axis=0, keepdims=True)

    def to_column(row):
        return jnp.sum(jnp.where(eye, row, 0.0), axis=1, keepdims=True)

    slots = slot_row[...]
    first_lane = lax.broadcasted_iota(jnp.int32, (1, TILE), 1)
    sources = [
        jnp.max(jnp.where(slots == e * TILES + s, first_lane, 0)) for s in range(TILES)
    ]
    gain_two = gain[pl.ds(2 * dp, 2)]
    gain_row = jnp.concatenate([gain_two[0:1], gain_two[1:2]], axis=1)

    def gather_copy(buf, sems, t, way):
        ref = buf.at[t, x]
        return remote(ref, ref, sems, (t, 0 if way > 0 else 1), device(dx=way))

    for s in range(TILES):
        picked = came_tiles[sources[s] // TILES].astype(F32)
        squares[dp, s : s + 1] = to_row(jnp.sum(picked * picked, axis=1, keepdims=True))
        rows_q[s, x] = (picked * gain_row).astype(BF)
        gather_copy(rows_q, gather_q_sem, s, 1).start()
        gather_copy(rows_q, gather_q_sem, s, -1).start()

    def sq_copy(i, j):
        ref = squares.at[dp]
        return remote(ref, ref, sq_sem, (i * SIDE + j,), device(dx=i, dy=j))

    for i, j in dp_steps:
        sq_copy(i, j).start()

    for i in (1, 3, 2):
        wo_copy(i).wait()
        wo_pair(i).start()

    def pass_copy(buf, sems, t, way):
        block = left_x if way > 0 else right_x
        part = pl.ds(0 if way > 0 else HALF, HALF)
        ref = buf.at[t, block, part]
        return remote(ref, ref, sems, (t, 0 if way > 0 else 1), device(dx=way))

    def pass_on(buf, first_sems, sems, t):
        gather_copy(buf, first_sems, t, 1).wait_recv()
        pass_copy(buf, sems, t, 1).start()
        gather_copy(buf, first_sems, t, -1).wait_recv()
        pass_copy(buf, sems, t, -1).start()

    def far_copy(far, half, sems, t, way):
        part = 0 if way > 0 else 1
        return remote(
            far.at[t, pl.ds(part * HALF, HALF)], half.at[t, part], sems, (t, part), device(dy=way)
        )

    def multiply(buf, sems, weight_block, kept, far, half, far_sems, t):
        pass_copy(buf, sems, t, 1).wait_recv()
        pass_copy(buf, sems, t, -1).wait_recv()
        rows = [buf[t, i] for i in range(SIDE)]

        def block(step):
            n = (y + step) % SIDE
            total = jnp.dot(rows[0], weight_block(0, n), preferred_element_type=F32)
            for i in range(1, SIDE):
                total = total + jnp.dot(rows[i], weight_block(i, n), preferred_element_type=F32)
            return total

        far[t] = block(2).astype(BF)
        far_copy(far, half, far_sems, t, 1).start()
        far_copy(far, half, far_sems, t, -1).start()
        kept[t, 0] = block(1)
        kept[t, 1] = block(3)
        kept[t, 2] = block(0)

    def near_copy(near, total, sems, t, way):
        part = 0 if way > 0 else 1
        return remote(near.at[t, part], total.at[t, part], sems, (t, part), device(dy=way))

    def add_far(kept, far, half, far_sems, near, total, near_sems, t):
        far_copy(far, half, far_sems, t, 1).wait_recv()
        near[t, 0, :HALF] = (kept[t, 0, :HALF] + half[t, 0].astype(F32)).astype(BF)
        near[t, 0, HALF:] = kept[t, 0, HALF:].astype(BF)
        near_copy(near, total, near_sems, t, 1).start()
        far_copy(far, half, far_sems, t, -1).wait_recv()
        near[t, 1, :HALF] = kept[t, 1, :HALF].astype(BF)
        near[t, 1, HALF:] = (kept[t, 1, HALF:] + half[t, 1].astype(F32)).astype(BF)
        near_copy(near, total, near_sems, t, -1).start()

    def finish(kept, near, total, near_sems, t):
        near_copy(near, total, near_sems, t, 1).wait_recv()
        near_copy(near, total, near_sems, t, -1).wait_recv()
        return kept[t, 2] + total[t, 0].astype(F32) + total[t, 1].astype(F32)

    def wq_block(i, n):
        return weight_q[n, i]

    def wo_block(i, n):
        return weight_o[i, :, pl.ds(pl.multiple_of(n * HD, HD), HD)]

    enc_row = jnp.concatenate([encoder_segment[i : i + 1] for i in range(ENC_PEERS)], axis=1)

    def attend(t):
        total = squares[0, pl.ds(t, 1)]
        for i in range(1, SIDE * SIDE):
            total = total + squares[i, pl.ds(t, 1)]
        scale = to_column(lax.rsqrt(total * (1.0 / FEATURES) + 1e-6))
        queries = (finish(kept_q, near_q, sum_q, near_q_sem, t) * scale).astype(BF)
        source = sources[0]
        for s in range(1, TILES):
            source = jnp.where(t == s, sources[s], source)
        segment = to_column(target_segment[pl.ds(source, 1)].astype(F32)).astype(jnp.int32)
        keys = kv[:, 0].reshape(ENC_PEERS * TILE, HD)
        values = kv[:, 1].reshape(ENC_PEERS * TILE, HD)
        scores = lax.dot_general(
            queries, keys, (((1,), (1,)), ((), ())), preferred_element_type=F32
        )
        allowed = segment == enc_row
        scores = jnp.where(allowed, scores, -1e30)
        top = jnp.max(scores, axis=-1, keepdims=True)
        weights = jnp.where(allowed, jnp.exp(scores - top), 0.0)
        denominator = jnp.sum(weights, axis=-1, keepdims=True)
        summed = jnp.dot(weights.astype(BF), values, preferred_element_type=F32)
        rows_o[t, x] = (summed / denominator).astype(BF)
        gather_copy(rows_o, gather_o_sem, t, 1).start()
        gather_copy(rows_o, gather_o_sem, t, -1).start()

    def out_copy(t):
        return pltpu.make_async_copy(
            out_rows.at[t], out.at[pl.ds(pl.multiple_of(t * TILE, TILE), TILE)], out_sem.at[t]
        )

    def kv_step(h):
        kv_copy(h - 1, 1).wait_recv()
        if h < 3:
            kv_copy(h, 1).start()
        else:
            kv_last(1).start()
        kv_pair(-h).start()
        kv_copy(h - 1, -1).wait_recv()
        if h < 3:
            kv_copy(h, -1).start()
        else:
            kv_last(-1).start()
        kv_pair(h).start()

    load_q.wait()
    load_o.wait()

    def turn(t, carry):
        for h in (1, 2, 3):

            @pl.when(t == h - 1)
            def _():
                kv_step(h)

        @pl.when(t < TILES)
        def _():
            pass_on(rows_q, gather_q_sem, pass_q_sem, t)

        @pl.when(t == 1)
        def _():
            for i in (1, 3, 2):
                wq_pair(i).wait()

        @pl.when((t >= 1) & (t < TILES + 1))
        def _():
            multiply(rows_q, pass_q_sem, wq_block, kept_q, far_q, half_q, far_q_sem, t - 1)

        @pl.when((t >= 2) & (t < TILES + 2))
        def _():
            add_far(kept_q, far_q, half_q, far_q_sem, near_q, sum_q, near_q_sem, t - 2)

        @pl.when(t == 3)
        def _():
            for i, j in dp_steps:
                sq_copy(i, j).wait()
            kv_last(1).wait_recv()
            kv_last(-1).wait_recv()
            kv_pair(4).start()
            for h in range(DEPTH):
                kv_pair(h).wait_recv()

        @pl.when((t >= 3) & (t < TILES + 3))
        def _():
            attend(t - 3)

        @pl.when((t >= 4) & (t < TILES + 4))
        def _():
            pass_on(rows_o, gather_o_sem, pass_o_sem, t - 4)

        @pl.when(t == 5)
        def _():
            for i in (1, 3, 2):
                wo_pair(i).wait()

        @pl.when((t >= 5) & (t < TILES + 5))
        def _():
            multiply(rows_o, pass_o_sem, wo_block, kept_o, far_o, half_o, far_o_sem, t - 5)

        @pl.when((t >= 6) & (t < TILES + 6))
        def _():
            add_far(kept_o, far_o, half_o, far_o_sem, near_o, sum_o, near_o_sem, t - 6)

        @pl.when((t >= 7) & (t < TILES + 7))
        def _():
            out_rows[t - 7] = finish(kept_o, near_o, sum_o, near_o_sem, t - 7).astype(BF)
            out_copy(t - 7).start()

        return carry

    lax.fori_loop(0, TILES + 7, turn, 0)

    for h in range(3):
        kv_copy(h, 1).wait_send()
        kv_copy(h, -1).wait_send()
    kv_last(1).wait_send()
    kv_last(-1).wait_send()
    for h in range(DEPTH):
        kv_pair(h).wait_send()

    def drain(t, carry):
        for way in (1, -1):
            gather_copy(rows_q, gather_q_sem, t, way).wait_send()
            gather_copy(rows_o, gather_o_sem, t, way).wait_send()
            pass_copy(rows_q, pass_q_sem, t, way).wait_send()
            pass_copy(rows_o, pass_o_sem, t, way).wait_send()
            far_copy(far_q, half_q, far_q_sem, t, way).wait_send()
            far_copy(far_o, half_o, far_o_sem, t, way).wait_send()
            near_copy(near_q, sum_q, near_q_sem, t, way).wait_send()
            near_copy(near_o, sum_o, near_o_sem, t, way).wait_send()
        out_copy(t).wait()
        return carry

    lax.fori_loop(0, TILES, drain, 0)


def local(
    targets,
    encoded,
    norm_gain,
    query_weight,
    key_weight,
    value_weight,
    output_weight,
    target_segment,
    encoder_segment,
    tile_slot,
):
    any_space = pl.BlockSpec(memory_space=pl.ANY)
    vmem = pl.BlockSpec(memory_space=pltpu.VMEM)
    smem = pl.BlockSpec(memory_space=pltpu.SMEM)
    sem = pltpu.SemaphoreType.DMA
    tile = (TILE, HD)
    scratch = [
        pltpu.VMEM((TILES,) + tile, BF),
        pltpu.VMEM((ENC_PEERS,) + tile, BF),
        pltpu.VMEM((ENC_PEERS,) + tile, BF),
        pltpu.VMEM((ENC_PEERS,) + tile, BF),
        pltpu.VMEM((ENC_PEERS, HD, HD), BF),
        pltpu.VMEM((ENC_PEERS, HD, HD), BF),
        pltpu.VMEM((SIDE, SIDE, HD, HD), BF),
        pltpu.VMEM((SIDE, HD, SIDE * HD), BF),
        pltpu.VMEM((ENC_PEERS, 2) + tile, BF),
        pltpu.VMEM((SIDE * SIDE, TILES, TILE), F32),
        pltpu.VMEM((TILES, SIDE) + tile, BF),
        pltpu.VMEM((TILES, SIDE) + tile, BF),
        pltpu.VMEM((TILES, 3) + tile, F32),
        pltpu.VMEM((TILES, 3) + tile, F32),
        pltpu.VMEM((TILES,) + tile, BF),
        pltpu.VMEM((TILES,) + tile, BF),
        pltpu.VMEM((TILES, 2, HALF, HD), BF),
        pltpu.VMEM((TILES, 2, HALF, HD), BF),
        pltpu.VMEM((TILES, 2) + tile, BF),
        pltpu.VMEM((TILES, 2) + tile, BF),
        pltpu.VMEM((TILES, 2) + tile, BF),
        pltpu.VMEM((TILES, 2) + tile, BF),
        pltpu.VMEM((TILES,) + tile, BF),
        sem((6,)),
        sem((2, SIDE * SIDE)),
        sem((2, ENC_PEERS)),
        sem((2, SIDE)),
        sem((2, SIDE)),
        sem((2, 2 * SIDE)),
        sem((2, 4, 2)),
        sem((2, DEPTH)),
        sem((2, SIDE * SIDE)),
        sem((2, TILES, 2)),
        sem((2, TILES, 2)),
        sem((2, TILES, 2)),
        sem((2, TILES, 2)),
        sem((2, TILES, 2)),
        sem((2, TILES, 2)),
        sem((2, TILES, 2)),
        sem((2, TILES, 2)),
        sem((TILES,)),
    ]
    return pl.pallas_call(
        kernel,
        out_shape=jax.ShapeDtypeStruct((TILES * TILE, HD), BF),
        in_specs=[any_space] * 2 + [vmem] + [any_space] * 4 + [vmem] * 3 + [smem],
        out_specs=any_space,
        scratch_shapes=scratch,
        compiler_params=pltpu.CompilerParams(
            collective_id=0, has_side_effects=True, vmem_limit_bytes=56 << 20
        ),
        cost_estimate=pl.CostEstimate(
            flops=7_000_000_000, bytes_accessed=10_000_000, transcendentals=2_000_000
        ),
        name="cross_attention",
    )(
        targets.reshape((TILES,) + tile),
        encoded,
        norm_gain.reshape(2 * SIDE * SIDE, TILE),
        query_weight.reshape(SIDE, SIDE, HD, HD),
        key_weight.reshape(ENC_PEERS, HD, HD),
        value_weight.reshape(ENC_PEERS, HD, HD),
        output_weight,
        target_segment.reshape(-1, TILE),
        encoder_segment.reshape(-1, TILE),
        tile_slot.reshape(1, -1),
        tile_slot,
    )


def solution(mesh):
    return jax.shard_map(
        local,
        mesh=mesh,
        in_specs=(
            P("enc", "dp"),
            P("enc", "dp"),
            P(),
            P(None, "dp"),
            P(None, "dp"),
            P(None, "dp"),
            P("dp", None),
            P(),
            P(),
            P(),
        ),
        out_specs=P("enc", "dp"),
        check_vma=False,
    )
```

time: 332 us -> 108 us (0.33)
  waiting for transfers between devices: 273 us -> 0 us
  Pallas kernels: 0 us -> 106 us
  matrix products: 20.6 us -> 0 us
  between operations: 13.8 us -> 0.01 us
  other arithmetic: 13 us -> 0 us
  local copies, waits for them, and re-layouts: 6.57 us -> 1.87 us
  starting transfers between devices: 4.43 us -> 0 us
    all_gather x3 -> x0, waiting for transfers between devices: 157 us -> none  [the longest x1 73.2 us: local(): lax.all_gather(targets, 'dp', axis=1, tiled=True)]
    pallas_call x0 -> x1, Pallas kernels: none -> 106 us  [local(): pl.pallas_call(kernel, out_shape=jax.ShapeDtypeStruct((TILES * TILE, HD),...]
    reduce_scatter x1 -> x0, waiting for transfers between devices: 88.9 us -> none  [local(): lax.psum_scatter(partial_out.astype(jnp.bfloat16), 'dp', scatter_dimensio...]
    all_to_all x1 -> x0, waiting for transfers between devices: 26.2 us -> none  [local(): lax.all_to_all(outgoing_tiles(home_context, send_match, enc_count), 'enc'...]
    dot_general x8 -> x0, matrix products: 20.6 us -> none  [the longest x1 5.57 us: local(): jnp.dot(context, output_weight, preferred_element_type=jnp.float32)]
    reduce_sum x3 -> x0, other arithmetic: 7.98 us -> none  [the longest x1 5.22 us: local(): jnp.mean(widened * widened, axis=-1, keepdims=True) + 1e-06]
    all_to_all x1 -> x0, starting transfers between devices: 4.13 us -> none  [local(): lax.all_to_all(outgoing_tiles(home_context, send_match, enc_count), 'enc'...]
  transfers between devices with their start and end apart: 5 -> 0, of which waited for: 5 -> 0; matrix products, arithmetic and copies ran while one was open for 7% -> 0% of each run, Pallas kernels for 0% -> 0%
where the time goes in v1:
time: 108 us
  Pallas kernels  106 us (98%)
  local copies, waits for them, and re-layouts  1.87 us (2%)
    pallas_call x1, Pallas kernels, local(): pl.pallas_call(kernel, out_shape=jax.ShapeDtypeStruct((TILES * TILE, HD),...  106 us

profile of v1, /device:TPU:8, one launch (start us, length us, event | category | flops | bytes accessed | tf_op | source)
XLA Modules:
  0.0 107.6 jit_solution(8656264532621809310)
XLA Ops:
  0.0 105.7 %cross_attention.1 = bf16[1024,256]{1,0:T(8,128)(2,1)} custom-call(bf16[8,128,256]{2,1,0:T(8,128)(2,1)} %bitcast.11, bf16[128,256]{1,0:T(8,128)(2,1)} %encoded.1, f32[32,128]{1,0:T(8,128)} %bitcast.13, bf16[4,4,256,256]{3,2,1,0:T(8,128)(2,1)} %bitcast.8, bf16[16,256,256]{2,1,0:T(8,128)(2,1)} %bitcast.9, bf16[16,256,256]{2,1,0:T(8,128)(2,1)} %bitcast.10, ...), custom_call_target="tpu_custom_call" | custom-call | flops 7000000000 | bytes 10000000 | tf_op jit(solution)/shard_map/cross_attention/pallas_call | solution.py:546
  105.7 1.9 %copy.12 = bf16[1024,256]{1,0:T(8,128)(2,1)} copy(bf16[1024,256]{1,0:T(8,128)(2,1)} %cross_attention.1) | data formatting | bytes 1048576

commit v2 on v1

--- a/solution.py
+++ b/solution.py
@@ -12,6 +12,8 @@
 SIDE = 4
 DEPTH = 8
 ENC_PEERS = 16
+AHEAD = 3
+LAG = 2
 FEATURES = 4096
 BF = jnp.bfloat16
 F32 = jnp.float32
@@ -124,22 +126,12 @@
         pl.semaphore_signal(
             barrier, inc=1, device_id=device(dz=i, dc=j), device_id_type=pl.DeviceIdType.MESH
         )
-    pl.semaphore_wait(barrier, len(dp_steps) + len(enc_steps))
-
-    def enc_copy(i, j):
-        return remote(
-            encoded, enc_all.at[dp], enc_sem, (i * SIDE + j,), device(dx=i, dy=j)
-        )
-
-    for i, j in dp_steps:
-        enc_copy(i, j).start()
-
     load_targets.wait()
     owners = [slot[e * TILES + i] // TILES for i in range(TILES)]
 
     def tile_copy(i, j):
         to = device(dz=i, dc=j)
-        return to[1], remote(
+        return remote(
             sent_tiles.at[i * 2 + j], came_tiles.at[e], tile_sem, (i * 2 + j,), to
         )
 
@@ -150,10 +142,20 @@
         return own_targets[found]
 
     for i, j in enc_steps:
-        peer, copy = tile_copy(i, j)
-        sent_tiles[i * 2 + j] = tile_for(peer)
-        copy.start()
+        sent_tiles[i * 2 + j] = tile_for(device(dz=i, dc=j)[1])
     came_tiles[e] = tile_for(e)
+
+    pl.semaphore_wait(barrier, len(dp_steps) + len(enc_steps))
+    for i, j in enc_steps:
+        tile_copy(i, j).start()
+
+    def enc_copy(i, j):
+        return remote(
+            encoded, enc_all.at[dp], enc_sem, (i * SIDE + j,), device(dx=i, dy=j)
+        )
+
+    for i, j in dp_steps:
+        enc_copy(i, j).start()
 
     def wq_copy(j):
         part = pl.ds(2 * c, 2)
@@ -175,14 +177,13 @@
             device(dx=i),
         )
 
+    load_encoded.wait()
+    for i, j in dp_steps:
+        enc_copy(i, j).wait()
     for i in (2, 1, 3):
         wq_copy(i).start()
     for i in (2, 1, 3):
         wo_copy(i).start()
-
-    load_encoded.wait()
-    for i, j in dp_steps:
-        enc_copy(i, j).wait()
     load_k.wait()
     load_v.wait()
 
@@ -243,7 +244,7 @@
         wq_pair(i).start()
 
     for i, j in enc_steps:
-        tile_copy(i, j)[1].wait()
+        tile_copy(i, j).wait()
 
     lanes = lax.broadcasted_iota(jnp.int32, (TILE, TILE), 1)
     eye = lax.broadcasted_iota(jnp.int32, (TILE, TILE), 0) == lanes
@@ -270,8 +271,9 @@
         picked = came_tiles[sources[s] // TILES].astype(F32)
         squares[dp, s : s + 1] = to_row(jnp.sum(picked * picked, axis=1, keepdims=True))
         rows_q[s, x] = (picked * gain_row).astype(BF)
-        gather_copy(rows_q, gather_q_sem, s, 1).start()
-        gather_copy(rows_q, gather_q_sem, s, -1).start()
+        if s < AHEAD:
+            gather_copy(rows_q, gather_q_sem, s, 1).start()
+            gather_copy(rows_q, gather_q_sem, s, -1).start()
 
     def sq_copy(i, j):
         ref = squares.at[dp]
@@ -396,68 +398,62 @@
     load_o.wait()
 
     def turn(t, carry):
-        for h in (1, 2, 3):
-
-            @pl.when(t == h - 1)
+        def stage(number, body):
+            tile = t - number * LAG
+
+            @pl.when((tile >= 0) & (tile < TILES))
             def _():
-                kv_step(h)
-
-        @pl.when(t < TILES)
-        def _():
-            pass_on(rows_q, gather_q_sem, pass_q_sem, t)
-
-        @pl.when(t == 1)
-        def _():
+                body(tile)
+
+        def once(at, body):
+            pl.when(t == at)(body)
+
+        def wait_wq():
             for i in (1, 3, 2):
                 wq_pair(i).wait()
 
-        @pl.when((t >= 1) & (t < TILES + 1))
-        def _():
-            multiply(rows_q, pass_q_sem, wq_block, kept_q, far_q, half_q, far_q_sem, t - 1)
-
-        @pl.when((t >= 2) & (t < TILES + 2))
-        def _():
-            add_far(kept_q, far_q, half_q, far_q_sem, near_q, sum_q, near_q_sem, t - 2)
-
-        @pl.when(t == 3)
-        def _():
-            for i, j in dp_steps:
-                sq_copy(i, j).wait()
+        def wait_wo():
+            for i in (1, 3, 2):
+                wo_pair(i).wait()
+
+        def last_kv():
             kv_last(1).wait_recv()
             kv_last(-1).wait_recv()
             kv_pair(4).start()
+
+        def wait_kv():
+            for i, j in dp_steps:
+                sq_copy(i, j).wait()
             for h in range(DEPTH):
                 kv_pair(h).wait_recv()
 
-        @pl.when((t >= 3) & (t < TILES + 3))
-        def _():
-            attend(t - 3)
-
-        @pl.when((t >= 4) & (t < TILES + 4))
-        def _():
-            pass_on(rows_o, gather_o_sem, pass_o_sem, t - 4)
-
-        @pl.when(t == 5)
-        def _():
-            for i in (1, 3, 2):
-                wo_pair(i).wait()
-
-        @pl.when((t >= 5) & (t < TILES + 5))
-        def _():
-            multiply(rows_o, pass_o_sem, wo_block, kept_o, far_o, half_o, far_o_sem, t - 5)
-
-        @pl.when((t >= 6) & (t < TILES + 6))
-        def _():
-            add_far(kept_o, far_o, half_o, far_o_sem, near_o, sum_o, near_o_sem, t - 6)
-
-        @pl.when((t >= 7) & (t < TILES + 7))
-        def _():
-            out_rows[t - 7] = finish(kept_o, near_o, sum_o, near_o_sem, t - 7).astype(BF)
-            out_copy(t - 7).start()
-
+        def next_gather():
+            gather_copy(rows_q, gather_q_sem, t + AHEAD, 1).start()
+            gather_copy(rows_q, gather_q_sem, t + AHEAD, -1).start()
+
+        def write(tile):
+            out_rows[tile] = finish(kept_o, near_o, sum_o, near_o_sem, tile).astype(BF)
+            out_copy(tile).start()
+
+        stage(0, lambda i: pass_on(rows_q, gather_q_sem, pass_q_sem, i))
+        pl.when(t < TILES - AHEAD)(next_gather)
+        once(LAG, wait_wq)
+        stage(1, lambda i: multiply(rows_q, pass_q_sem, wq_block, kept_q, far_q, half_q, far_q_sem, i))
+        stage(2, lambda i: add_far(kept_q, far_q, half_q, far_q_sem, near_q, sum_q, near_q_sem, i))
+        once(1, lambda: kv_step(2))
+        once(3, lambda: kv_step(3))
+        once(5, last_kv)
+        once(3 * LAG, wait_kv)
+        stage(3, attend)
+        stage(4, lambda i: pass_on(rows_o, gather_o_sem, pass_o_sem, i))
+        once(5 * LAG, wait_wo)
+        stage(5, lambda i: multiply(rows_o, pass_o_sem, wo_block, kept_o, far_o, half_o, far_o_sem, i))
+        stage(6, lambda i: add_far(kept_o, far_o, half_o, far_o_sem, near_o, sum_o, near_o_sem, i))
+        stage(7, write)
         return carry
 
-    lax.fori_loop(0, TILES + 7, turn, 0)
+    kv_step(1)
+    lax.fori_loop(0, TILES + 7 * LAG, turn, 0)
 
     for h in range(3):
         kv_copy(h, 1).wait_send()

time: 108 us -> 97.3 us (0.901)
  Pallas kernels: 106 us -> 94.7 us
    pallas_call x1, Pallas kernels: 106 us -> 94.7 us  [local(): pl.pallas_call(kernel, out_shape=jax.ShapeDtypeStruct((TILES * TILE, HD),...]
where the time goes in v2:
time: 97.3 us; the launch traced here: 96.6 us
  Pallas kernels  94.7 us (97%)
  local copies, waits for them, and re-layouts  1.87 us (2%)
    pallas_call x1, Pallas kernels, local(): pl.pallas_call(kernel, out_shape=jax.ShapeDtypeStruct((TILES * TILE, HD),...  94.7 us

profile of v2, /device:TPU:8, one launch (start us, length us, event | category | flops | bytes accessed | tf_op | source)
XLA Modules:
  0.0 96.6 jit_solution(930121676785699183)
XLA Ops:
  0.0 94.7 %cross_attention.1 = bf16[1024,256]{1,0:T(8,128)(2,1)} custom-call(bf16[8,128,256]{2,1,0:T(8,128)(2,1)} %bitcast.11, bf16[128,256]{1,0:T(8,128)(2,1)} %encoded.1, f32[32,128]{1,0:T(8,128)} %bitcast.13, bf16[4,4,256,256]{3,2,1,0:T(8,128)(2,1)} %bitcast.8, bf16[16,256,256]{2,1,0:T(8,128)(2,1)} %bitcast.9, bf16[16,256,256]{2,1,0:T(8,128)(2,1)} %bitcast.10, ...), custom_call_target="tpu_custom_call" | custom-call | flops 7000000000 | bytes 10000000 | tf_op jit(solution)/shard_map/cross_attention/pallas_call | solution.py:542
  94.7 1.9 %copy.12 = bf16[1024,256]{1,0:T(8,128)(2,1)} copy(bf16[1024,256]{1,0:T(8,128)(2,1)} %cross_attention.1) | data formatting | bytes 1048576

commit v3 on v2

--- a/solution.py
+++ b/solution.py
@@ -12,8 +12,8 @@
 SIDE = 4
 DEPTH = 8
 ENC_PEERS = 16
-AHEAD = 3
-LAG = 2
+BATCH = 4
+GROUP = 5
 FEATURES = 4096
 BF = jnp.bfloat16
 F32 = jnp.float32
@@ -55,6 +55,8 @@
     sum_q,
     sum_o,
     out_rows,
+    out_tiles,
+    kv_total,
     local_sem,
     enc_sem,
     tile_sem,
@@ -98,7 +100,7 @@
     right_x, left_x = (x + 1) % SIDE, (x + 3) % SIDE
     far_x = (x + 2) % SIDE
     dp_steps = [(i, j) for i in (2, 1, 3, 0) for j in (2, 1, 3, 0) if (i, j) != (0, 0)]
-    enc_steps = [(i, j) for i in (4, 3, 5, 2, 6, 1, 7, 0) for j in (0, 1) if (i, j) != (0, 0)]
+    enc_steps = [(i, j) for i in (0, 1, 7, 2, 6, 3, 5, 4) for j in (0, 1)][1:]
 
     load_targets = pltpu.make_async_copy(targets, own_targets, local_sem.at[0])
     load_encoded = pltpu.make_async_copy(encoded, enc_all.at[dp], local_sem.at[1])
@@ -129,10 +131,10 @@
     load_targets.wait()
     owners = [slot[e * TILES + i] // TILES for i in range(TILES)]
 
-    def tile_copy(i, j):
-        to = device(dz=i, dc=j)
+    def tile_copy(rank):
+        i, j = enc_steps[rank - 1]
         return remote(
-            sent_tiles.at[i * 2 + j], came_tiles.at[e], tile_sem, (i * 2 + j,), to
+            sent_tiles.at[rank], came_tiles.at[rank], tile_sem, (rank,), device(dz=i, dc=j)
         )
 
     def tile_for(peer):
@@ -141,13 +143,14 @@
             found = jnp.where(owners[i] == peer, i, found)
         return own_targets[found]
 
-    for i, j in enc_steps:
-        sent_tiles[i * 2 + j] = tile_for(device(dz=i, dc=j)[1])
-    came_tiles[e] = tile_for(e)
+    for rank in range(1, ENC_PEERS):
+        i, j = enc_steps[rank - 1]
+        sent_tiles[rank] = tile_for(device(dz=i, dc=j)[1])
+    came_tiles[0] = tile_for(e)
 
     pl.semaphore_wait(barrier, len(dp_steps) + len(enc_steps))
-    for i, j in enc_steps:
-        tile_copy(i, j).start()
+    for rank in range(1, ENC_PEERS):
+        tile_copy(rank).start()
 
     def enc_copy(i, j):
         return remote(
@@ -177,27 +180,39 @@
             device(dx=i),
         )
 
-    load_encoded.wait()
-    for i, j in dp_steps:
-        enc_copy(i, j).wait()
-    for i in (2, 1, 3):
-        wq_copy(i).start()
-    for i in (2, 1, 3):
-        wo_copy(i).start()
     load_k.wait()
     load_v.wait()
-
-    def project(block, sums):
+    load_encoded.wait()
+
+    def project(block):
         rows = enc_all[block]
         return (
-            sums[0] + jnp.dot(rows, weight_k[block], preferred_element_type=F32),
-            sums[1] + jnp.dot(rows, weight_v[block], preferred_element_type=F32),
-        )
-
-    zero = jnp.zeros((TILE, HD), F32)
-    key_rows, value_rows = lax.fori_loop(0, ENC_PEERS, project, (zero, zero))
-    kv[e, 0] = key_rows.astype(BF)
-    kv[e, 1] = value_rows.astype(BF)
+            jnp.dot(rows, weight_k[block], preferred_element_type=F32),
+            jnp.dot(rows, weight_v[block], preferred_element_type=F32),
+        )
+
+    def add_blocks(blocks):
+        key_part, value_part = project(blocks[0])
+        for block in blocks[1:]:
+            more = project(block)
+            key_part, value_part = key_part + more[0], value_part + more[1]
+        return key_part, value_part
+
+    kv_total[0], kv_total[1] = add_blocks([dp])
+    for first in range(0, len(dp_steps), GROUP):
+        group = dp_steps[first : first + GROUP]
+        for i, j in group:
+            enc_copy(i, j).wait_recv()
+        if first == 0:
+            for i in (2, 1, 3):
+                wq_copy(i).start()
+            for i in (2, 1, 3):
+                wo_copy(i).start()
+        parts = add_blocks([device(dx=-i, dy=-j)[0] for i, j in group])
+        kv_total[0] += parts[0]
+        kv_total[1] += parts[1]
+    kv[e, 0] = kv_total[0].astype(BF)
+    kv[e, 1] = kv_total[1].astype(BF)
 
     def kv_block(step):
         return ((z + step + DEPTH) % DEPTH) * 2 + c
@@ -239,13 +254,6 @@
         ref = weight_o.at[block, part]
         return remote(ref, ref, pair_sem, (SIDE + i,), device(dc=1))
 
-    for i in (1, 3, 2):
-        wq_copy(i).wait()
-        wq_pair(i).start()
-
-    for i, j in enc_steps:
-        tile_copy(i, j).wait()
-
     lanes = lax.broadcasted_iota(jnp.int32, (TILE, TILE), 1)
     eye = lax.broadcasted_iota(jnp.int32, (TILE, TILE), 0) == lanes
 
@@ -257,9 +265,31 @@
 
     slots = slot_row[...]
     first_lane = lax.broadcasted_iota(jnp.int32, (1, TILE), 1)
-    sources = [
+    slot_sources = [
         jnp.max(jnp.where(slots == e * TILES + s, first_lane, 0)) for s in range(TILES)
     ]
+
+    def rank_of(source):
+        home = source // TILES
+        gap = (z - home // 2 + DEPTH) % DEPTH
+        place = jnp.where(gap <= DEPTH // 2, jnp.maximum(2 * gap - 1, 0), 2 * (DEPTH - gap))
+        return 2 * place + jnp.where(home % 2 == c, 0, 1)
+
+    ranks = [rank_of(source) for source in slot_sources]
+    places = []
+    for s in range(TILES):
+        place = jnp.int32(0)
+        for other in range(TILES):
+            if other != s:
+                place = place + jnp.where(ranks[other] < ranks[s], 1, 0)
+        places.append(place)
+
+    def of_tile(values, t):
+        value = jnp.int32(0)
+        for s in range(TILES):
+            value = jnp.where(places[s] == t, values[s], value)
+        return value
+
     gain_two = gain[pl.ds(2 * dp, 2)]
     gain_row = jnp.concatenate([gain_two[0:1], gain_two[1:2]], axis=1)
 
@@ -267,24 +297,22 @@
         ref = buf.at[t, x]
         return remote(ref, ref, sems, (t, 0 if way > 0 else 1), device(dx=way))
 
-    for s in range(TILES):
-        picked = came_tiles[sources[s] // TILES].astype(F32)
-        squares[dp, s : s + 1] = to_row(jnp.sum(picked * picked, axis=1, keepdims=True))
-        rows_q[s, x] = (picked * gain_row).astype(BF)
-        if s < AHEAD:
-            gather_copy(rows_q, gather_q_sem, s, 1).start()
-            gather_copy(rows_q, gather_q_sem, s, -1).start()
-
-    def sq_copy(i, j):
-        ref = squares.at[dp]
-        return remote(ref, ref, sq_sem, (i * SIDE + j,), device(dx=i, dy=j))
-
-    for i, j in dp_steps:
-        sq_copy(i, j).start()
-
-    for i in (1, 3, 2):
-        wo_copy(i).wait()
-        wo_pair(i).start()
+    def pick(t):
+        rank = of_tile(ranks, t)
+        picked = came_tiles[t]
+        for more in range(1, TILES + 1):
+            picked = jnp.where(rank == t + more, came_tiles[t + more], picked)
+        picked = picked.astype(F32)
+        rows_q[t, x] = (picked * gain_row).astype(BF)
+        gather_copy(rows_q, gather_q_sem, t, 1).start()
+        gather_copy(rows_q, gather_q_sem, t, -1).start()
+        squares[t // BATCH, dp, pl.ds(t % BATCH, 1)] = to_row(
+            jnp.sum(picked * picked, axis=1, keepdims=True)
+        )
+
+    def sq_copy(batch, i, j):
+        ref = squares.at[batch, dp]
+        return remote(ref, ref, sq_sem, (batch, i * SIDE + j), device(dx=i, dy=j))
 
     def pass_copy(buf, sems, t, way):
         block = left_x if way > 0 else right_x
@@ -351,15 +379,13 @@
     enc_row = jnp.concatenate([encoder_segment[i : i + 1] for i in range(ENC_PEERS)], axis=1)
 
     def attend(t):
-        total = squares[0, pl.ds(t, 1)]
+        batch, row = t // BATCH, pl.ds(t % BATCH, 1)
+        total = squares[batch, 0, row]
         for i in range(1, SIDE * SIDE):
-            total = total + squares[i, pl.ds(t, 1)]
+            total = total + squares[batch, i, row]
         scale = to_column(lax.rsqrt(total * (1.0 / FEATURES) + 1e-6))
         queries = (finish(kept_q, near_q, sum_q, near_q_sem, t) * scale).astype(BF)
-        source = sources[0]
-        for s in range(1, TILES):
-            source = jnp.where(t == s, sources[s], source)
-        segment = to_column(target_segment[pl.ds(source, 1)].astype(F32)).astype(jnp.int32)
+        segment = to_column(target_segment[pl.ds(of_tile(slot_sources, t), 1)].astype(F32)).astype(jnp.int32)
         keys = kv[:, 0].reshape(ENC_PEERS * TILE, HD)
         values = kv[:, 1].reshape(ENC_PEERS * TILE, HD)
         scores = lax.dot_general(
@@ -377,7 +403,7 @@
 
     def out_copy(t):
         return pltpu.make_async_copy(
-            out_rows.at[t], out.at[pl.ds(pl.multiple_of(t * TILE, TILE), TILE)], out_sem.at[t]
+            out_tiles.at[t], out.at[pl.ds(pl.multiple_of(t * TILE, TILE), TILE)], out_sem.at[t]
         )
 
     def kv_step(h):
@@ -398,8 +424,8 @@
     load_o.wait()
 
     def turn(t, carry):
-        def stage(number, body):
-            tile = t - number * LAG
+        def stage(late, body):
+            tile = t - late
 
             @pl.when((tile >= 0) & (tile < TILES))
             def _():
@@ -407,6 +433,16 @@
 
         def once(at, body):
             pl.when(t == at)(body)
+
+        def pass_wq():
+            for i in (1, 3, 2):
+                wq_copy(i).wait()
+                wq_pair(i).start()
+
+        def pass_wo():
+            for i in (1, 3, 2):
+                wo_copy(i).wait()
+                wo_pair(i).start()
 
         def wait_wq():
             for i in (1, 3, 2):
@@ -422,39 +458,58 @@
             kv_pair(4).start()
 
         def wait_kv():
-            for i, j in dp_steps:
-                sq_copy(i, j).wait()
             for h in range(DEPTH):
                 kv_pair(h).wait_recv()
 
-        def next_gather():
-            gather_copy(rows_q, gather_q_sem, t + AHEAD, 1).start()
-            gather_copy(rows_q, gather_q_sem, t + AHEAD, -1).start()
+        def send_squares(batch):
+            for i, j in dp_steps:
+                sq_copy(batch, i, j).start()
+
+        def wait_squares(batch):
+            for i, j in dp_steps:
+                sq_copy(batch, i, j).wait()
 
         def write(tile):
             out_rows[tile] = finish(kept_o, near_o, sum_o, near_o_sem, tile).astype(BF)
-            out_copy(tile).start()
-
-        stage(0, lambda i: pass_on(rows_q, gather_q_sem, pass_q_sem, i))
-        pl.when(t < TILES - AHEAD)(next_gather)
-        once(LAG, wait_wq)
-        stage(1, lambda i: multiply(rows_q, pass_q_sem, wq_block, kept_q, far_q, half_q, far_q_sem, i))
-        stage(2, lambda i: add_far(kept_q, far_q, half_q, far_q_sem, near_q, sum_q, near_q_sem, i))
-        once(1, lambda: kv_step(2))
-        once(3, lambda: kv_step(3))
-        once(5, last_kv)
-        once(3 * LAG, wait_kv)
-        stage(3, attend)
-        stage(4, lambda i: pass_on(rows_o, gather_o_sem, pass_o_sem, i))
-        once(5 * LAG, wait_wo)
-        stage(5, lambda i: multiply(rows_o, pass_o_sem, wo_block, kept_o, far_o, half_o, far_o_sem, i))
-        stage(6, lambda i: add_far(kept_o, far_o, half_o, far_o_sem, near_o, sum_o, near_o_sem, i))
-        stage(7, write)
+
+        for tile in range(1, TILES):
+            once(tile, tile_copy(TILES + tile).wait_recv)
+        stage(0, pick)
+        for batch in (0, 1):
+            once((batch + 1) * BATCH - 1, lambda batch=batch: send_squares(batch))
+        once(1, lambda: kv_step(1))
+        once(2, pass_wq)
+        stage(2, lambda i: pass_on(rows_q, gather_q_sem, pass_q_sem, i))
+        once(3, lambda: kv_step(2))
+        stage(5, lambda i: add_far(kept_q, far_q, half_q, far_q_sem, near_q, sum_q, near_q_sem, i))
+        once(5, lambda: kv_step(3))
+        once(7, last_kv)
+        once(7, wait_kv)
+        for batch in (0, 1):
+            once(7 + batch * BATCH, lambda batch=batch: wait_squares(batch))
+        stage(7, attend)
+        once(6, pass_wo)
+        stage(9, lambda i: pass_on(rows_o, gather_o_sem, pass_o_sem, i))
+        stage(12, lambda i: add_far(kept_o, far_o, half_o, far_o_sem, near_o, sum_o, near_o_sem, i))
+        stage(14, write)
+        once(3, wait_wq)
+        stage(3, lambda i: multiply(rows_q, pass_q_sem, wq_block, kept_q, far_q, half_q, far_q_sem, i))
+        once(10, wait_wo)
+        stage(10, lambda i: multiply(rows_o, pass_o_sem, wo_block, kept_o, far_o, half_o, far_o_sem, i))
         return carry
 
-    kv_step(1)
-    lax.fori_loop(0, TILES + 7 * LAG, turn, 0)
-
+    for rank in range(1, TILES + 1):
+        tile_copy(rank).wait_recv()
+    lax.fori_loop(0, TILES + 14, turn, 0)
+
+    for s in range(TILES):
+        out_tiles[s] = out_rows[places[s]]
+        out_copy(s).start()
+
+    for rank in range(1, ENC_PEERS):
+        tile_copy(rank).wait_send()
+    for i, j in dp_steps:
+        enc_copy(i, j).wait_send()
     for h in range(3):
         kv_copy(h, 1).wait_send()
         kv_copy(h, -1).wait_send()
@@ -506,7 +561,7 @@
         pltpu.VMEM((SIDE, SIDE, HD, HD), BF),
         pltpu.VMEM((SIDE, HD, SIDE * HD), BF),
         pltpu.VMEM((ENC_PEERS, 2) + tile, BF),
-        pltpu.VMEM((SIDE * SIDE, TILES, TILE), F32),
+        pltpu.VMEM((2, SIDE * SIDE, TILES, TILE), F32),
         pltpu.VMEM((TILES, SIDE) + tile, BF),
         pltpu.VMEM((TILES, SIDE) + tile, BF),
         pltpu.VMEM((TILES, 3) + tile, F32),
@@ -520,6 +575,8 @@
         pltpu.VMEM((TILES, 2) + tile, BF),
         pltpu.VMEM((TILES, 2) + tile, BF),
         pltpu.VMEM((TILES,) + tile, BF),
+        pltpu.VMEM((TILES,) + tile, BF),
+        pltpu.VMEM((2,) + tile, F32),
         sem((6,)),
         sem((2, SIDE * SIDE)),
         sem((2, ENC_PEERS)),
@@ -528,7 +585,7 @@
         sem((2, 2 * SIDE)),
         sem((2, 4, 2)),
         sem((2, DEPTH)),
-        sem((2, SIDE * SIDE)),
+        sem((2, 2, SIDE * SIDE)),
         sem((2, TILES, 2)),
         sem((2, TILES, 2)),
         sem((2, TILES, 2)),

time: 97.3 us -> 100 us (1.028)
  Pallas kernels: 94.7 us -> 98.4 us
    pallas_call x1, Pallas kernels: 94.7 us -> 98.4 us  [local(): pl.pallas_call(kernel, out_shape=jax.ShapeDtypeStruct((TILES * TILE, HD),...]
where the time goes in v3:
time: 100 us
  Pallas kernels  98.4 us (98%)
  local copies, waits for them, and re-layouts  1.87 us (2%)
    pallas_call x1, Pallas kernels, local(): pl.pallas_call(kernel, out_shape=jax.ShapeDtypeStruct((TILES * TILE, HD),...  98.4 us

profile of v3, /device:TPU:8, one launch (start us, length us, event | category | flops | bytes accessed | tf_op | source)
XLA Modules:
  0.0 100.3 jit_solution(6878594430912731467)
XLA Ops:
  0.0 98.4 %cross_attention.1 = bf16[1024,256]{1,0:T(8,128)(2,1)} custom-call(bf16[8,128,256]{2,1,0:T(8,128)(2,1)} %bitcast.11, bf16[128,256]{1,0:T(8,128)(2,1)} %encoded.1, f32[32,128]{1,0:T(8,128)} %bitcast.13, bf16[4,4,256,256]{3,2,1,0:T(8,128)(2,1)} %bitcast.8, bf16[16,256,256]{2,1,0:T(8,128)(2,1)} %bitcast.9, bf16[16,256,256]{2,1,0:T(8,128)(2,1)} %bitcast.10, ...), custom_call_target="tpu_custom_call" | custom-call | flops 7000000000 | bytes 10000000 | tf_op jit(solution)/shard_map/cross_attention/pallas_call | solution.py:599
  98.4 1.9 %copy.12 = bf16[1024,256]{1,0:T(8,128)(2,1)} copy(bf16[1024,256]{1,0:T(8,128)(2,1)} %cross_attention.1) | data formatting | bytes 1048576

commit v4 on v3

--- a/solution.py
+++ b/solution.py
@@ -13,7 +13,7 @@
 DEPTH = 8
 ENC_PEERS = 16
 BATCH = 4
-GROUP = 5
+NEAR = 10
 FEATURES = 4096
 BF = jnp.bfloat16
 F32 = jnp.float32
@@ -56,7 +56,6 @@
     sum_o,
     out_rows,
     out_tiles,
-    kv_total,
     local_sem,
     enc_sem,
     tile_sem,
@@ -103,7 +102,7 @@
     enc_steps = [(i, j) for i in (0, 1, 7, 2, 6, 3, 5, 4) for j in (0, 1)][1:]
 
     load_targets = pltpu.make_async_copy(targets, own_targets, local_sem.at[0])
-    load_encoded = pltpu.make_async_copy(encoded, enc_all.at[dp], local_sem.at[1])
+    load_encoded = pltpu.make_async_copy(encoded, enc_all.at[x, y], local_sem.at[1])
     load_k = pltpu.make_async_copy(key_weight, weight_k, local_sem.at[2])
     load_v = pltpu.make_async_copy(value_weight, weight_v, local_sem.at[3])
     load_q = pltpu.make_async_copy(query_weight.at[:, y], weight_q.at[y], local_sem.at[4])
@@ -149,16 +148,31 @@
     came_tiles[0] = tile_for(e)
 
     pl.semaphore_wait(barrier, len(dp_steps) + len(enc_steps))
-    for rank in range(1, ENC_PEERS):
+    for rank in range(1, NEAR):
         tile_copy(rank).start()
 
-    def enc_copy(i, j):
-        return remote(
-            encoded, enc_all.at[dp], enc_sem, (i * SIDE + j,), device(dx=i, dy=j)
-        )
-
-    for i, j in dp_steps:
-        enc_copy(i, j).start()
+    upper, lower = pl.ds(0, HALF), pl.ds(HALF, HALF)
+
+    def enc_first(i):
+        return (
+            remote(
+                encoded.at[upper], enc_all.at[x, y, upper], enc_sem, (0, i), device(dx=i)
+            ),
+            remote(
+                encoded.at[lower], enc_all.at[x, y, lower], enc_sem, (1, i), device(dy=i)
+            ),
+        )
+
+    def enc_second(i):
+        column, line = enc_all.at[:, y, upper], enc_all.at[x, :, lower]
+        return (
+            remote(column, column, enc_sem, (2, i), device(dy=i)),
+            remote(line, line, enc_sem, (3, i), device(dx=i)),
+        )
+
+    for i in (2, 1, 3):
+        for copy in enc_first(i):
+            copy.start()
 
     def wq_copy(j):
         part = pl.ds(2 * c, 2)
@@ -180,39 +194,36 @@
             device(dx=i),
         )
 
+    load_encoded.wait()
+    for i in (1, 3, 2):
+        for copy in enc_first(i):
+            copy.wait_recv()
+    for i in (2, 1, 3):
+        for copy in enc_second(i):
+            copy.start()
+    for i in (2, 1, 3):
+        wq_copy(i).start()
+        wo_copy(i).start()
+
     load_k.wait()
     load_v.wait()
-    load_encoded.wait()
-
-    def project(block):
-        rows = enc_all[block]
-        return (
-            jnp.dot(rows, weight_k[block], preferred_element_type=F32),
-            jnp.dot(rows, weight_v[block], preferred_element_type=F32),
-        )
-
-    def add_blocks(blocks):
-        key_part, value_part = project(blocks[0])
-        for block in blocks[1:]:
-            more = project(block)
-            key_part, value_part = key_part + more[0], value_part + more[1]
-        return key_part, value_part
-
-    kv_total[0], kv_total[1] = add_blocks([dp])
-    for first in range(0, len(dp_steps), GROUP):
-        group = dp_steps[first : first + GROUP]
-        for i, j in group:
-            enc_copy(i, j).wait_recv()
-        if first == 0:
-            for i in (2, 1, 3):
-                wq_copy(i).start()
-            for i in (2, 1, 3):
-                wo_copy(i).start()
-        parts = add_blocks([device(dx=-i, dy=-j)[0] for i, j in group])
-        kv_total[0] += parts[0]
-        kv_total[1] += parts[1]
-    kv[e, 0] = kv_total[0].astype(BF)
-    kv[e, 1] = kv_total[1].astype(BF)
+    for i in (1, 3, 2):
+        for copy in enc_second(i):
+            copy.wait_recv()
+
+    def project(weight):
+        total = jnp.zeros((TILE, HD), F32)
+        for i in range(SIDE):
+            part = jnp.zeros((TILE, HD), F32)
+            for j in range(SIDE):
+                part = part + jnp.dot(
+                    enc_all[i, j], weight[i * SIDE + j], preferred_element_type=F32
+                )
+            total = total + part
+        return total.astype(BF)
+
+    kv[e, 0] = project(weight_k)
+    kv[e, 1] = project(weight_v)
 
     def kv_block(step):
         return ((z + step + DEPTH) % DEPTH) * 2 + c
@@ -241,6 +252,8 @@
     kv_copy(0, 1).start()
     kv_copy(0, -1).start()
     kv_pair(0).start()
+    for rank in (10, 12):
+        tile_copy(rank).start()
 
     def wq_pair(j):
         block = (y + SIDE - j) % SIDE
@@ -406,7 +419,7 @@
             out_tiles.at[t], out.at[pl.ds(pl.multiple_of(t * TILE, TILE), TILE)], out_sem.at[t]
         )
 
-    def kv_step(h):
+    def kv_step(h, far_ranks):
         kv_copy(h - 1, 1).wait_recv()
         if h < 3:
             kv_copy(h, 1).start()
@@ -419,6 +432,8 @@
         else:
             kv_last(-1).start()
         kv_pair(h).start()
+        for rank in far_ranks:
+            tile_copy(rank).start()
 
     load_q.wait()
     load_o.wait()
@@ -477,30 +492,30 @@
         stage(0, pick)
         for batch in (0, 1):
             once((batch + 1) * BATCH - 1, lambda batch=batch: send_squares(batch))
-        once(1, lambda: kv_step(1))
+        once(1, lambda: kv_step(1, (11, 13)))
         once(2, pass_wq)
         stage(2, lambda i: pass_on(rows_q, gather_q_sem, pass_q_sem, i))
-        once(3, lambda: kv_step(2))
+        once(3, lambda: kv_step(2, (14, 15)))
         stage(5, lambda i: add_far(kept_q, far_q, half_q, far_q_sem, near_q, sum_q, near_q_sem, i))
-        once(5, lambda: kv_step(3))
+        once(5, lambda: kv_step(3, ()))
         once(7, last_kv)
-        once(7, wait_kv)
+        once(8, wait_kv)
         for batch in (0, 1):
-            once(7 + batch * BATCH, lambda batch=batch: wait_squares(batch))
-        stage(7, attend)
+            once(8 + batch * BATCH, lambda batch=batch: wait_squares(batch))
+        stage(8, attend)
         once(6, pass_wo)
-        stage(9, lambda i: pass_on(rows_o, gather_o_sem, pass_o_sem, i))
-        stage(12, lambda i: add_far(kept_o, far_o, half_o, far_o_sem, near_o, sum_o, near_o_sem, i))
-        stage(14, write)
+        stage(10, lambda i: pass_on(rows_o, gather_o_sem, pass_o_sem, i))
+        stage(13, lambda i: add_far(kept_o, far_o, half_o, far_o_sem, near_o, sum_o, near_o_sem, i))
+        stage(15, write)
         once(3, wait_wq)
         stage(3, lambda i: multiply(rows_q, pass_q_sem, wq_block, kept_q, far_q, half_q, far_q_sem, i))
-        once(10, wait_wo)
-        stage(10, lambda i: multiply(rows_o, pass_o_sem, wo_block, kept_o, far_o, half_o, far_o_sem, i))
+        once(11, wait_wo)
+        stage(11, lambda i: multiply(rows_o, pass_o_sem, wo_block, kept_o, far_o, half_o, far_o_sem, i))
         return carry
 
     for rank in range(1, TILES + 1):
         tile_copy(rank).wait_recv()
-    lax.fori_loop(0, TILES + 14, turn, 0)
+    lax.fori_loop(0, TILES + 15, turn, 0)
 
     for s in range(TILES):
         out_tiles[s] = out_rows[places[s]]
@@ -508,8 +523,9 @@
 
     for rank in range(1, ENC_PEERS):
         tile_copy(rank).wait_send()
-    for i, j in dp_steps:
-        enc_copy(i, j).wait_send()
+    for i in (1, 2, 3):
+        for copy in enc_first(i) + enc_second(i):
+            copy.wait_send()
     for h in range(3):
         kv_copy(h, 1).wait_send()
         kv_copy(h, -1).wait_send()
@@ -555,7 +571,7 @@
         pltpu.VMEM((TILES,) + tile, BF),
         pltpu.VMEM((ENC_PEERS,) + tile, BF),
         pltpu.VMEM((ENC_PEERS,) + tile, BF),
-        pltpu.VMEM((ENC_PEERS,) + tile, BF),
+        pltpu.VMEM((SIDE, SIDE) + tile, BF),
         pltpu.VMEM((ENC_PEERS, HD, HD), BF),
         pltpu.VMEM((ENC_PEERS, HD, HD), BF),
         pltpu.VMEM((SIDE, SIDE, HD, HD), BF),
@@ -576,9 +592,8 @@
         pltpu.VMEM((TILES, 2) + tile, BF),
         pltpu.VMEM((TILES,) + tile, BF),
         pltpu.VMEM((TILES,) + tile, BF),
-        pltpu.VMEM((2,) + tile, F32),
         sem((6,)),
-        sem((2, SIDE * SIDE)),
+        sem((2, 4, SIDE)),
         sem((2, ENC_PEERS)),
         sem((2, SIDE)),
         sem((2, SIDE)),

time: 100 us -> 104 us (1.040); the launches traced: 100 us -> 102 us
  Pallas kernels: 98.4 us -> 100 us
    pallas_call x1, Pallas kernels: 98.4 us -> 100 us  [local(): pl.pallas_call(kernel, out_shape=jax.ShapeDtypeStruct((TILES * TILE, HD),...]
where the time goes in v4:
time: 104 us; the launch traced here: 102 us
  Pallas kernels  100 us (96%)
  local copies, waits for them, and re-layouts  1.87 us (2%)
    pallas_call x1, Pallas kernels, local(): pl.pallas_call(kernel, out_shape=jax.ShapeDtypeStruct((TILES * TILE, HD),...  100 us

profile of v4, /device:TPU:8, one launch (start us, length us, event | category | flops | bytes accessed | tf_op | source)
XLA Modules:
  0.0 102.2 jit_solution(13547656055479291451)
XLA Ops:
  0.0 100.3 %cross_attention.1 = bf16[1024,256]{1,0:T(8,128)(2,1)} custom-call(bf16[8,128,256]{2,1,0:T(8,128)(2,1)} %bitcast.11, bf16[128,256]{1,0:T(8,128)(2,1)} %encoded.1, f32[32,128]{1,0:T(8,128)} %bitcast.13, bf16[4,4,256,256]{3,2,1,0:T(8,128)(2,1)} %bitcast.8, bf16[16,256,256]{2,1,0:T(8,128)(2,1)} %bitcast.9, bf16[16,256,256]{2,1,0:T(8,128)(2,1)} %bitcast.10, ...), custom_call_target="tpu_custom_call" | custom-call | flops 7000000000 | bytes 10000000 | tf_op jit(solution)/shard_map/cross_attention/pallas_call | solution.py:614
  100.3 1.9 %copy.12 = bf16[1024,256]{1,0:T(8,128)(2,1)} copy(bf16[1024,256]{1,0:T(8,128)(2,1)} %cross_attention.1) | data formatting | bytes 1048576

commit v5 on v4

--- a/solution.py
+++ b/solution.py
@@ -12,8 +12,10 @@
 SIDE = 4
 DEPTH = 8
 ENC_PEERS = 16
-BATCH = 4
+BATCH = 8
 NEAR = 10
+SPLIT = 32
+ATTEND = 8
 FEATURES = 4096
 BF = jnp.bfloat16
 F32 = jnp.float32
@@ -113,10 +115,6 @@
     )
     load_targets.start()
     load_encoded.start()
-    load_k.start()
-    load_v.start()
-    load_q.start()
-    load_o.start()
 
     barrier = pltpu.get_barrier_semaphore()
     for i, j in dp_steps:
@@ -151,7 +149,7 @@
     for rank in range(1, NEAR):
         tile_copy(rank).start()
 
-    upper, lower = pl.ds(0, HALF), pl.ds(HALF, HALF)
+    upper, lower = pl.ds(0, SPLIT), pl.ds(SPLIT, TILE - SPLIT)
 
     def enc_first(i):
         return (
@@ -194,6 +192,10 @@
             device(dx=i),
         )
 
+    load_k.start()
+    load_v.start()
+    load_q.start()
+    load_o.start()
     load_encoded.wait()
     for i in (1, 3, 2):
         for copy in enc_first(i):
@@ -204,6 +206,8 @@
     for i in (2, 1, 3):
         wq_copy(i).start()
         wo_copy(i).start()
+    for rank in range(NEAR, ENC_PEERS):
+        tile_copy(rank).start()
 
     load_k.wait()
     load_v.wait()
@@ -222,38 +226,23 @@
             total = total + part
         return total.astype(BF)
 
-    kv[e, 0] = project(weight_k)
-    kv[e, 1] = project(weight_v)
-
     def kv_block(step):
         return ((z + step + DEPTH) % DEPTH) * 2 + c
 
-    def kv_copy(step, way):
+    def kv_copy(step, way, part):
         block = kv_block(-step * way)
-        return remote(
-            kv.at[block],
-            kv.at[block],
-            kv_sem,
-            (step, 0 if way > 0 else 1),
-            device(dz=way),
-        )
-
-    def kv_last(way):
-        block = kv_block(-3 * way)
-        part = 0 if way > 0 else 1
-        return remote(
-            kv.at[block, part], kv.at[block, part], kv_sem, (3, part), device(dz=way)
-        )
+        ref = kv.at[block, part]
+        return remote(ref, ref, kv_sem, (step, 0 if way > 0 else 1, part), device(dz=way))
 
     def kv_pair(step):
         block = kv_block(step)
         return remote(kv.at[block], kv.at[block], kvp_sem, ((step + DEPTH) % DEPTH,), device(dc=1))
 
-    kv_copy(0, 1).start()
-    kv_copy(0, -1).start()
+    for part, weight in ((0, weight_k), (1, weight_v)):
+        kv[e, part] = project(weight)
+        kv_copy(0, 1, part).start()
+        kv_copy(0, -1, part).start()
     kv_pair(0).start()
-    for rank in (10, 12):
-        tile_copy(rank).start()
 
     def wq_pair(j):
         block = (y + SIDE - j) % SIDE
@@ -407,7 +396,7 @@
         allowed = segment == enc_row
         scores = jnp.where(allowed, scores, -1e30)
         top = jnp.max(scores, axis=-1, keepdims=True)
-        weights = jnp.where(allowed, jnp.exp(scores - top), 0.0)
+        weights = jnp.exp(scores - top)
         denominator = jnp.sum(weights, axis=-1, keepdims=True)
         summed = jnp.dot(weights.astype(BF), values, preferred_element_type=F32)
         rows_o[t, x] = (summed / denominator).astype(BF)
@@ -419,24 +408,14 @@
             out_tiles.at[t], out.at[pl.ds(pl.multiple_of(t * TILE, TILE), TILE)], out_sem.at[t]
         )
 
-    def kv_step(h, far_ranks):
-        kv_copy(h - 1, 1).wait_recv()
-        if h < 3:
-            kv_copy(h, 1).start()
-        else:
-            kv_last(1).start()
+    def kv_step(h):
+        for part in (0, 1):
+            for way in (1, -1):
+                kv_copy(h - 1, way, part).wait_recv()
+                if h < 3 or part == (0 if way > 0 else 1):
+                    kv_copy(h, way, part).start()
         kv_pair(-h).start()
-        kv_copy(h - 1, -1).wait_recv()
-        if h < 3:
-            kv_copy(h, -1).start()
-        else:
-            kv_last(-1).start()
         kv_pair(h).start()
-        for rank in far_ranks:
-            tile_copy(rank).start()
-
-    load_q.wait()
-    load_o.wait()
 
     def turn(t, carry):
         def stage(late, body):
@@ -460,16 +439,18 @@
                 wo_pair(i).start()
 
         def wait_wq():
+            load_q.wait()
             for i in (1, 3, 2):
                 wq_pair(i).wait()
 
         def wait_wo():
+            load_o.wait()
             for i in (1, 3, 2):
                 wo_pair(i).wait()
 
         def last_kv():
-            kv_last(1).wait_recv()
-            kv_last(-1).wait_recv()
+            kv_copy(3, 1, 0).wait_recv()
+            kv_copy(3, -1, 1).wait_recv()
             kv_pair(4).start()
 
         def wait_kv():
@@ -490,32 +471,32 @@
         for tile in range(1, TILES):
             once(tile, tile_copy(TILES + tile).wait_recv)
         stage(0, pick)
-        for batch in (0, 1):
+        for batch in range(TILES // BATCH):
             once((batch + 1) * BATCH - 1, lambda batch=batch: send_squares(batch))
-        once(1, lambda: kv_step(1, (11, 13)))
         once(2, pass_wq)
         stage(2, lambda i: pass_on(rows_q, gather_q_sem, pass_q_sem, i))
-        once(3, lambda: kv_step(2, (14, 15)))
-        stage(5, lambda i: add_far(kept_q, far_q, half_q, far_q_sem, near_q, sum_q, near_q_sem, i))
-        once(5, lambda: kv_step(3, ()))
+        once(4, wait_wq)
+        stage(4, lambda i: multiply(rows_q, pass_q_sem, wq_block, kept_q, far_q, half_q, far_q_sem, i))
+        stage(6, lambda i: add_far(kept_q, far_q, half_q, far_q_sem, near_q, sum_q, near_q_sem, i))
+        once(2, lambda: kv_step(1))
+        once(4, lambda: kv_step(2))
+        once(6, lambda: kv_step(3))
         once(7, last_kv)
-        once(8, wait_kv)
-        for batch in (0, 1):
-            once(8 + batch * BATCH, lambda batch=batch: wait_squares(batch))
-        stage(8, attend)
-        once(6, pass_wo)
-        stage(10, lambda i: pass_on(rows_o, gather_o_sem, pass_o_sem, i))
-        stage(13, lambda i: add_far(kept_o, far_o, half_o, far_o_sem, near_o, sum_o, near_o_sem, i))
-        stage(15, write)
-        once(3, wait_wq)
-        stage(3, lambda i: multiply(rows_q, pass_q_sem, wq_block, kept_q, far_q, half_q, far_q_sem, i))
-        once(11, wait_wo)
-        stage(11, lambda i: multiply(rows_o, pass_o_sem, wo_block, kept_o, far_o, half_o, far_o_sem, i))
+        once(ATTEND, wait_kv)
+        for batch in range(TILES // BATCH):
+            once(ATTEND + batch * BATCH, lambda batch=batch: wait_squares(batch))
+        stage(ATTEND, attend)
+        once(7, pass_wo)
+        stage(ATTEND + 2, lambda i: pass_on(rows_o, gather_o_sem, pass_o_sem, i))
+        once(ATTEND + 4, wait_wo)
+        stage(ATTEND + 4, lambda i: multiply(rows_o, pass_o_sem, wo_block, kept_o, far_o, half_o, far_o_sem, i))
+        stage(ATTEND + 6, lambda i: add_far(kept_o, far_o, half_o, far_o_sem, near_o, sum_o, near_o_sem, i))
+        stage(ATTEND + 8, write)
         return carry
 
     for rank in range(1, TILES + 1):
         tile_copy(rank).wait_recv()
-    lax.fori_loop(0, TILES + 15, turn, 0)
+    lax.fori_loop(0, TILES + ATTEND + 8, turn, 0)
 
     for s in range(TILES):
         out_tiles[s] = out_rows[places[s]]
@@ -527,10 +508,11 @@
         for copy in enc_first(i) + enc_second(i):
             copy.wait_send()
     for h in range(3):
-        kv_copy(h, 1).wait_send()
-        kv_copy(h, -1).wait_send()
-    kv_last(1).wait_send()
-    kv_last(-1).wait_send()
+        for part in (0, 1):
+            kv_copy(h, 1, part).wait_send()
+            kv_copy(h, -1, part).wait_send()
+    kv_copy(3, 1, 0).wait_send()
+    kv_copy(3, -1, 1).wait_send()
     for h in range(DEPTH):
         kv_pair(h).wait_send()
 
@@ -577,7 +559,7 @@
         pltpu.VMEM((SIDE, SIDE, HD, HD), BF),
         pltpu.VMEM((SIDE, HD, SIDE * HD), BF),
         pltpu.VMEM((ENC_PEERS, 2) + tile, BF),
-        pltpu.VMEM((2, SIDE * SIDE, TILES, TILE), F32),
+        pltpu.VMEM((TILES // BATCH, SIDE * SIDE, TILES, TILE), F32),
         pltpu.VMEM((TILES, SIDE) + tile, BF),
         pltpu.VMEM((TILES, SIDE) + tile, BF),
         pltpu.VMEM((TILES, 3) + tile, F32),
@@ -598,9 +580,9 @@
         sem((2, SIDE)),
         sem((2, SIDE)),
         sem((2, 2 * SIDE)),
-        sem((2, 4, 2)),
+        sem((2, 4, 2, 2)),
         sem((2, DEPTH)),
-        sem((2, 2, SIDE * SIDE)),
+        sem((2, TILES // BATCH, SIDE * SIDE)),
         sem((2, TILES, 2)),
         sem((2, TILES, 2)),
         sem((2, TILES, 2)),

time: 104 us -> 95.8 us (0.921); the launches traced: 102 us -> 95.6 us
  Pallas kernels: 100 us -> 93.7 us
    pallas_call x1, Pallas kernels: 100 us -> 93.7 us  [local(): pl.pallas_call(kernel, out_shape=jax.ShapeDtypeStruct((TILES * TILE, HD),...]
where the time goes in v5:
time: 95.8 us; the launch traced here: 95.6 us
  Pallas kernels  93.7 us (98%)
  local copies, waits for them, and re-layouts  1.87 us (2%)
    pallas_call x1, Pallas kernels, local(): pl.pallas_call(kernel, out_shape=jax.ShapeDtypeStruct((TILES * TILE, HD),...  93.7 us

profile of v5, /device:TPU:8, one launch (start us, length us, event | category | flops | bytes accessed | tf_op | source)
XLA Modules:
  0.0 95.6 jit_solution(9693758132716189525)
XLA Ops:
  0.0 93.7 %cross_attention.1 = bf16[1024,256]{1,0:T(8,128)(2,1)} custom-call(bf16[8,128,256]{2,1,0:T(8,128)(2,1)} %bitcast.11, bf16[128,256]{1,0:T(8,128)(2,1)} %encoded.1, f32[32,128]{1,0:T(8,128)} %bitcast.13, bf16[4,4,256,256]{3,2,1,0:T(8,128)(2,1)} %bitcast.8, bf16[16,256,256]{2,1,0:T(8,128)(2,1)} %bitcast.9, bf16[16,256,256]{2,1,0:T(8,128)(2,1)} %bitcast.10, ...), custom_call_target="tpu_custom_call" | custom-call | flops 7000000000 | bytes 10000000 | tf_op jit(solution)/shard_map/cross_attention/pallas_call | solution.py:596
  93.7 1.9 %copy.12 = bf16[1024,256]{1,0:T(8,128)(2,1)} copy(bf16[1024,256]{1,0:T(8,128)(2,1)} %cross_attention.1) | data formatting | bytes 1048576

commit v6 on v5

--- a/solution.py
+++ b/solution.py
@@ -125,29 +125,7 @@
         pl.semaphore_signal(
             barrier, inc=1, device_id=device(dz=i, dc=j), device_id_type=pl.DeviceIdType.MESH
         )
-    load_targets.wait()
-    owners = [slot[e * TILES + i] // TILES for i in range(TILES)]
-
-    def tile_copy(rank):
-        i, j = enc_steps[rank - 1]
-        return remote(
-            sent_tiles.at[rank], came_tiles.at[rank], tile_sem, (rank,), device(dz=i, dc=j)
-        )
-
-    def tile_for(peer):
-        found = jnp.int32(0)
-        for i in range(1, TILES):
-            found = jnp.where(owners[i] == peer, i, found)
-        return own_targets[found]
-
-    for rank in range(1, ENC_PEERS):
-        i, j = enc_steps[rank - 1]
-        sent_tiles[rank] = tile_for(device(dz=i, dc=j)[1])
-    came_tiles[0] = tile_for(e)
-
     pl.semaphore_wait(barrier, len(dp_steps) + len(enc_steps))
-    for rank in range(1, NEAR):
-        tile_copy(rank).start()
 
     upper, lower = pl.ds(0, SPLIT), pl.ds(SPLIT, TILE - SPLIT)
 
@@ -171,6 +149,28 @@
     for i in (2, 1, 3):
         for copy in enc_first(i):
             copy.start()
+
+    load_targets.wait()
+    owners = [slot[e * TILES + i] // TILES for i in range(TILES)]
+
+    def tile_copy(rank):
+        i, j = enc_steps[rank - 1]
+        return remote(
+            sent_tiles.at[rank], came_tiles.at[rank], tile_sem, (rank,), device(dz=i, dc=j)
+        )
+
+    def tile_for(peer):
+        found = jnp.int32(0)
+        for i in range(1, TILES):
+            found = jnp.where(owners[i] == peer, i, found)
+        return own_targets[found]
+
+    for rank in range(1, ENC_PEERS):
+        i, j = enc_steps[rank - 1]
+        sent_tiles[rank] = tile_for(device(dz=i, dc=j)[1])
+        if rank < NEAR:
+            tile_copy(rank).start()
+    came_tiles[0] = tile_for(e)
 
     def wq_copy(j):
         part = pl.ds(2 * c, 2)

time: 95.8 us -> 95.8 us (level)
  no operation moved by 1% of the time
where the time goes in v6:
time: 95.8 us; the launch traced here: 95.6 us
  Pallas kernels  93.7 us (98%)
  local copies, waits for them, and re-layouts  1.87 us (2%)
    pallas_call x1, Pallas kernels, local(): pl.pallas_call(kernel, out_shape=jax.ShapeDtypeStruct((TILES * TILE, HD),...  93.7 us

profile of v6, /device:TPU:8, one launch (start us, length us, event | category | flops | bytes accessed | tf_op | source)
XLA Modules:
  0.0 95.6 jit_solution(16494422973225187441)
XLA Ops:
  0.0 93.7 %cross_attention.1 = bf16[1024,256]{1,0:T(8,128)(2,1)} custom-call(bf16[8,128,256]{2,1,0:T(8,128)(2,1)} %bitcast.11, bf16[128,256]{1,0:T(8,128)(2,1)} %encoded.1, f32[32,128]{1,0:T(8,128)} %bitcast.13, bf16[4,4,256,256]{3,2,1,0:T(8,128)(2,1)} %bitcast.8, bf16[16,256,256]{2,1,0:T(8,128)(2,1)} %bitcast.9, bf16[16,256,256]{2,1,0:T(8,128)(2,1)} %bitcast.10, ...), custom_call_target="tpu_custom_call" | custom-call | flops 7000000000 | bytes 10000000 | tf_op jit(solution)/shard_map/cross_attention/pallas_call | solution.py:596
  93.7 1.9 %copy.12 = bf16[1024,256]{1,0:T(8,128)(2,1)} copy(bf16[1024,256]{1,0:T(8,128)(2,1)} %cross_attention.1) | data formatting | bytes 1048576

commit v7 on v6

--- a/solution.py
+++ b/solution.py
@@ -14,7 +14,7 @@
 ENC_PEERS = 16
 BATCH = 8
 NEAR = 10
-SPLIT = 32
+SPLIT = 16
 ATTEND = 8
 FEATURES = 4096
 BF = jnp.bfloat16

time: 95.8 us -> 97.4 us (1.017)
  Pallas kernels: 93.7 us -> 95.3 us
    pallas_call x1, Pallas kernels: 93.7 us -> 95.3 us  [local(): pl.pallas_call(kernel, out_shape=jax.ShapeDtypeStruct((TILES * TILE, HD),...]
where the time goes in v7:
time: 97.4 us; the launch traced here: 97.2 us
  Pallas kernels  95.3 us (98%)
  local copies, waits for them, and re-layouts  1.87 us (2%)
    pallas_call x1, Pallas kernels, local(): pl.pallas_call(kernel, out_shape=jax.ShapeDtypeStruct((TILES * TILE, HD),...  95.3 us

profile of v7, /device:TPU:8, one launch (start us, length us, event | category | flops | bytes accessed | tf_op | source)
XLA Modules:
  0.0 97.2 jit_solution(1216232191613190928)
XLA Ops:
  0.0 95.3 %cross_attention.1 = bf16[1024,256]{1,0:T(8,128)(2,1)} custom-call(bf16[8,128,256]{2,1,0:T(8,128)(2,1)} %bitcast.11, bf16[128,256]{1,0:T(8,128)(2,1)} %encoded.1, f32[32,128]{1,0:T(8,128)} %bitcast.13, bf16[4,4,256,256]{3,2,1,0:T(8,128)(2,1)} %bitcast.8, bf16[16,256,256]{2,1,0:T(8,128)(2,1)} %bitcast.9, bf16[16,256,256]{2,1,0:T(8,128)(2,1)} %bitcast.10, ...), custom_call_target="tpu_custom_call" | custom-call | flops 7000000000 | bytes 10000000 | tf_op jit(solution)/shard_map/cross_attention/pallas_call | solution.py:596
  95.3 1.9 %copy.12 = bf16[1024,256]{1,0:T(8,128)(2,1)} copy(bf16[1024,256]{1,0:T(8,128)(2,1)} %cross_attention.1) | data formatting | bytes 1048576
